TPU v7x, 128 devices: a whole 4x4x4 slice. The times are simulated.
128 devices in a mesh: lat: 4 (over z_lo, core), lon: 32 (over x, z_hi, y).
Axes of the slice: x: 4, y: 4, z: 4 (z_hi: 2, z_lo: 2; z = z_hi * 2 + z_lo), core: 2. Of those that a mesh axis runs over, the one named last changes fastest.
Arguments:
- in_field: bfloat16 [256, 1440, 256], P('lat', 'lon'), may hold values from -6 to 6
- out_grad: bfloat16 [256, 1440, 256], P('lat', 'lon'), may hold values from -6 to 6
- spec_weight: bfloat16 [4096, 2, 16, 256], P(('lat', 'lon')), may hold values from -1 to 1
- inner_weight: bfloat16 [256, 1024], replicated, may hold values from -0.375 to 0.375
- output_projection_weight: bfloat16 [1024, 256], replicated, may hold values from -0.1875 to 0.1875
- kept_modes: int32 [4096], P(('lat', 'lon')), may hold values from 0 to 63, as said below
Outputs:
- input_grad: bfloat16 [256, 1440, 256], P('lat', 'lon')
- spectral_grad: float32 [4096, 2, 16, 256], P(('lat', 'lon'))
Inputs may be any that keep to these rules, and one draw needn't show every extreme that they name: `kept_modes`: the 32 entries of each aligned block of 32 are distinct; entry v names the mode v // 2 of the block's latitude wavenumbers and v mod 2 of its longitude wavenumbers.
All inputs are finite; a program needn't handle non-finite values.
Results may differ from a plain program's by a relative error of at most 0.029.
Values may be sent and summed in bfloat16 or wider, within the bound.
A program may use at most 128 MiB of HBM per device.

v0:
```python
import math

import jax
import jax.numpy as jnp
from jax import lax
from jax.sharding import PartitionSpec as P

BS = 16
KM = 64
KLAT = 128


def from_partner(value, axis, bit):
    return lax.ppermute(value, axis, [(i, i ^ 1 << bit) for i in range(lax.axis_size(axis))])


def make_lon_basis(lon_total, blocks):
    lon_ids = jnp.arange(lon_total, dtype=jnp.int32)
    mode_ids = jnp.arange(KM, dtype=jnp.int32)
    phases = lon_ids[:, None] * mode_ids[None, :] % lon_total
    angles = phases.astype(jnp.float32) * (2.0 * math.pi / lon_total)
    basis = jnp.stack([jnp.cos(angles), -jnp.sin(angles)], axis=1).astype(jnp.bfloat16)
    basis = basis.reshape(lon_total, 2, blocks, KM // blocks)
    return jnp.transpose(basis, (0, 2, 1, 3)).reshape(lon_total, 2 * KM)


def lat_basis(doubled_rows, wave_ids, lat_total):
    wavenum = wave_ids - KLAT // 2
    phases = jnp.mod(wavenum[None, :, None] * doubled_rows[:, None, :], 2 * lat_total)
    angles = phases.astype(jnp.float32) * (math.pi / lat_total)
    return (jnp.cos(angles).astype(jnp.bfloat16), jnp.sin(angles).astype(jnp.bfloat16))


def with_mirror(row_ids, halves, lat_total):
    if halves == 1:
        return row_ids[None]
    return jnp.stack([row_ids, 2 * lat_total - 1 - row_ids])


def lat_analysis_term(spectrum, cos_tab, sin_tab):
    with_cos = jnp.einsum("hkr,hrpmc->kpmc", cos_tab, spectrum, preferred_element_type=jnp.float32)
    with_sin = jnp.einsum("hkr,hrpmc->kpmc", sin_tab, spectrum, preferred_element_type=jnp.float32)
    return jnp.stack([with_cos[:, 0] + with_sin[:, 1], with_cos[:, 1] - with_sin[:, 0]], axis=1)


def lat_synthesis_term(portion, cos_tab, sin_tab):
    with_cos = jnp.einsum("hkr,kpmc->hrpmc", cos_tab, portion, preferred_element_type=jnp.float32)
    with_sin = jnp.einsum("hkr,kpmc->hrpmc", sin_tab, portion, preferred_element_type=jnp.float32)
    return jnp.stack(
        [with_cos[:, :, 0] - with_sin[:, :, 1], with_sin[:, :, 0] + with_cos[:, :, 1]], axis=2
    )


def body(in_field, out_grad, spec_weight, inner_weight, output_projection_weight, kept_modes):
    lat_parts = lax.axis_size("lat")
    lon_parts = lax.axis_size("lon")
    lat_dev, lon_dev, channels = in_field.shape
    keep_count = kept_modes.shape[0]
    blocks_mix = channels // BS
    lat_total = lat_dev * lat_parts
    lon_total = lon_dev * lon_parts
    mode_block = KM // lon_parts
    wave_block = KLAT // lat_parts
    fwd_scale = 1.0 / math.sqrt(2 * lat_total * lon_total)
    syn_scale = 1.0 / math.sqrt(keep_count * lat_parts * lon_parts)
    longitude_basis = make_lon_basis(lon_total, lon_parts)
    latitude_rank = lax.axis_index("lat")
    my_rows = latitude_rank * lat_dev + jnp.arange(lat_dev, dtype=jnp.int32)
    highest = lax.Precision.HIGHEST

    def regather(tile_row_slice):
        return lax.all_to_all(tile_row_slice, "lon", split_axis=2, concat_axis=1, tiled=True)

    def transposed(grid_point_values, inner):
        return inner(
            lax.all_to_all(grid_point_values, "lon", split_axis=1, concat_axis=2, tiled=True)
        )

    def turn(grid_point_values):
        return from_partner(grid_point_values, "lon", lon_parts.bit_length() - 2)

    def lon_spectrum(row_grid):
        spectrum = jnp.einsum(
            "hrjc,jq->hrqc", row_grid, longitude_basis, preferred_element_type=jnp.float32
        )
        return regather(spectrum.astype(jnp.bfloat16))

    def lat_section(spectrum, halves, scale):
        spectrum = spectrum.reshape(halves, lat_dev, 2, mode_block, channels)
        wave_ids = jnp.arange(wave_block * lax.axis_size("lat"), dtype=jnp.int32)
        cos_tab, sin_tab = lat_basis(with_mirror(my_rows, halves, lat_total), wave_ids, lat_total)
        reduced_total = lax.psum_scatter(
            lat_analysis_term(spectrum, cos_tab, sin_tab).astype(jnp.bfloat16),
            "lat",
            scatter_dimension=0,
            tiled=True,
        ).astype(jnp.float32)
        return reduced_total * scale

    def pick(reduced_total):
        flat_modes = jnp.transpose(reduced_total, (0, 2, 1, 3)).reshape(
            wave_block * mode_block, 2, channels
        )
        return jnp.take(flat_modes, kept_modes, axis=0)

    def place(values):
        flat_modes = (
            jnp.zeros((wave_block * mode_block, 2, channels), values.dtype)
            .at[kept_modes]
            .set(values)
        )
        return jnp.transpose(flat_modes.reshape(wave_block, mode_block, 2, channels), (0, 2, 1, 3))

    def synthesize(values, halves, finish):
        placed = place(values)
        portion = lax.all_gather(placed, "lat", axis=0, tiled=True)
        wave_ids = jnp.arange(portion.shape[0], dtype=jnp.int32)
        cos_tab, sin_tab = lat_basis(with_mirror(my_rows, halves, lat_total), wave_ids, lat_total)
        row_spec = lat_synthesis_term(portion, cos_tab, sin_tab)
        row_spec = row_spec.astype(jnp.bfloat16).reshape(halves, lat_dev, 2 * mode_block, channels)

        def lon_inverse(tile_row_slice):
            grid_point_values = jnp.einsum(
                "hrqc,jq->hrjc", tile_row_slice, longitude_basis, preferred_element_type=jnp.float32
            )
            return regather(finish(grid_point_values))

        return transposed(row_spec, lon_inverse)

    partner = turn(in_field)
    forward_spectrum_layout = transposed(jnp.stack([in_field, partner]), lon_spectrum)
    modes_in = pick(lat_section(forward_spectrum_layout, 2, fwd_scale))
    weights = spec_weight.astype(jnp.float32).reshape(keep_count, 2, blocks_mix, BS, BS)
    in_parts = modes_in.reshape(keep_count, 2, blocks_mix, BS)
    real_part = jnp.einsum(
        "qbi,qbio->qbo", in_parts[:, 0], weights[:, 0], precision=highest
    ) - jnp.einsum("qbi,qbio->qbo", in_parts[:, 1], weights[:, 1], precision=highest)
    imag_part = jnp.einsum(
        "qbi,qbio->qbo", in_parts[:, 0], weights[:, 1], precision=highest
    ) + jnp.einsum("qbi,qbio->qbo", in_parts[:, 1], weights[:, 0], precision=highest)
    mixed_modes = (
        jnp.stack([real_part, imag_part], axis=1)
        .reshape(keep_count, 2, channels)
        .astype(jnp.bfloat16)
    )

    def finish_out(grid_point_values):
        return (grid_point_values * syn_scale).astype(jnp.bfloat16)

    grid_out = synthesize(mixed_modes, 1, finish_out)[0]
    points = lat_dev * lon_dev
    pre_act = jnp.dot(
        grid_out.reshape(points, channels), inner_weight, preferred_element_type=jnp.float32
    )
    unused, pullback = jax.vjp(jax.nn.gelu, pre_act)
    hidden_grad = jnp.dot(
        out_grad.reshape(points, channels),
        output_projection_weight.T,
        preferred_element_type=jnp.float32,
    )
    pre_grad = pullback(hidden_grad)[0].astype(jnp.bfloat16)
    grid_grad = jnp.dot(pre_grad, inner_weight.T, preferred_element_type=jnp.float32).astype(
        jnp.bfloat16
    )
    grid_grad = grid_grad.reshape(lat_dev, lon_dev, channels)
    back_spec = transposed(grid_grad[None], lon_spectrum)
    modes_grad = pick(lat_section(back_spec, 1, syn_scale))
    grad_parts = modes_grad.reshape(keep_count, 2, blocks_mix, BS)
    weight_real = jnp.einsum(
        "qbi,qbo->qbio", in_parts[:, 0], grad_parts[:, 0], precision=highest
    ) + jnp.einsum("qbi,qbo->qbio", in_parts[:, 1], grad_parts[:, 1], precision=highest)
    weight_imag = jnp.einsum(
        "qbi,qbo->qbio", in_parts[:, 0], grad_parts[:, 1], precision=highest
    ) - jnp.einsum("qbi,qbo->qbio", in_parts[:, 1], grad_parts[:, 0], precision=highest)
    spectral_grad = jnp.stack([weight_real, weight_imag], axis=1).reshape(
        keep_count, 2, blocks_mix, BS * BS
    )
    back_real = jnp.einsum(
        "qbo,qbio->qbi", grad_parts[:, 0], weights[:, 0], precision=highest
    ) + jnp.einsum("qbo,qbio->qbi", grad_parts[:, 1], weights[:, 1], precision=highest)
    back_imag = jnp.einsum(
        "qbo,qbio->qbi", grad_parts[:, 1], weights[:, 0], precision=highest
    ) - jnp.einsum("qbo,qbio->qbi", grad_parts[:, 0], weights[:, 1], precision=highest)
    mode_back = (
        jnp.stack([back_real, back_imag], axis=1)
        .reshape(keep_count, 2, channels)
        .astype(jnp.bfloat16)
    )

    def keep_halves(grid_point_values):
        return (grid_point_values * fwd_scale).astype(jnp.bfloat16)

    halves_grid = synthesize(mode_back, 2, keep_halves)
    lower_turned = turn(halves_grid[1])
    spectral_part = (halves_grid[0].astype(jnp.float32) + lower_turned.astype(jnp.float32)).astype(
        jnp.bfloat16
    )
    input_grad = (out_grad.astype(jnp.float32) + spectral_part.astype(jnp.float32)).astype(
        jnp.bfloat16
    )
    return (input_grad, spectral_grad)


def solution(mesh):
    return jax.shard_map(
        body,
        mesh=mesh,
        in_specs=(
            P("lat", "lon", None),
            P("lat", "lon", None),
            P(("lat", "lon"), None, None, None),
            P(),
            P(),
            P(("lat", "lon")),
        ),
        out_specs=(P("lat", "lon", None), P(("lat", "lon"), None, None, None)),
        check_vma=False,
    )
```

profile of v0, /device:TPU:0, one launch (start us, length us, event | category | flops | bytes accessed | tf_op | source)
XLA Modules:
  0.0 430.5 jit_solution(5759912060302464126)
XLA Ops:
  10.4 32.5 %collective-permute-done = bf16[64,45,256]{2,0,1:T(8,128)(2,1)S(1)} collective-permute-done((bf16[64,45,256]{2,0,1:T(8,128)(2,1)}, bf16[64,45,256]{2,0,1:T(8,128)(2,1)S(1)}, u32[]{:S(2)}, u32[]{:S(2)}) %collective-permute-start) | collective-permute-done | bytes 1474592 | tf_op jit(solution)/shard_map/ppermute | solution.py:14
  44.5 4.7 %copy.187 = bf16[2,64,45,256]{3,0,2,1:T(2,128)(2,1)} copy(bf16[2,64,45,256]{3,1,2,0:T(8,128)(2,1)S(1)} %pad_maximum_fusion) | data formatting | bytes 5898240 | tf_op jit(solution)/shard_map/stack | solution.py:131
  49.2 11.0 %all-to-all-start = ((bf16[2,64,45,256]{3,0,2,1:T(2,128)(2,1)}), bf16[2,64,45,256]{3,0,2,1:T(2,128)(2,1)}, u32[]{:S(2)}, u32[]{:S(2)}) async-start(bf16[2,64,45,256]{3,0,2,1:T(2,128)(2,1)} %copy.187), calls=%async_computation | async-start | bytes 5898240 | tf_op jit(solution)/shard_map/all_to_all | solution.py:76
  62.8 36.6 %all-to-all-done = bf16[2,64,45,256]{3,0,2,1:T(2,128)(2,1)} async-done(((bf16[2,64,45,256]{3,0,2,1:T(2,128)(2,1)}), bf16[2,64,45,256]{3,0,2,1:T(2,128)(2,1)}, u32[]{:S(2)}, u32[]{:S(2)}) %all-to-all-start) | async-done | bytes 2949152 | tf_op jit(solution)/shard_map/all_to_all | solution.py:76
  105.0 6.3 %all-to-all-start.1 = ((bf16[2,2,128,256]{3,1,0,2:T(2,128)(2,1)}), bf16[2,2,128,256]{3,1,0,2:T(2,128)(2,1)S(1)}, u32[]{:S(2)}, u32[]{:S(2)}) async-start(bf16[2,2,128,256]{3,1,0,2:T(2,128)(2,1)} %copy.191), calls=%async_computation.1 | async-start | bytes 524288 | tf_op jit(solution)/shard_map/all_to_all | solution.py:72
  113.9 8.1 %all-to-all-done.1 = bf16[2,2,128,256]{3,1,0,2:T(2,128)(2,1)S(1)} async-done(((bf16[2,2,128,256]{3,1,0,2:T(2,128)(2,1)}), bf16[2,2,128,256]{3,1,0,2:T(2,128)(2,1)S(1)}, u32[]{:S(2)}, u32[]{:S(2)}) %all-to-all-start.1) | async-done | bytes 262176 | tf_op jit(solution)/shard_map/all_to_all | solution.py:72
  124.4 12.9 %reduce-scatter.3.cloned.1.call-done = bf16[32,2,2,256]{3,0,2,1:T(8,128)(2,1)} async-done(((bf16[128,2,2,256]{3,0,2,1:T(8,128)(2,1)}), bf16[32,2,2,256]{3,0,2,1:T(8,128)(2,1)}) %reduce-scatter.3.cloned.1.call-update) | async-done | bytes 65552 | tf_op jit(solution)/shard_map/reduce_scatter | solution.py:92
  143.7 5.9 %all_gather.6 = bf16[128,2,2,256]{3,0,2,1:T(8,128)(2,1)S(1)} all-gather(bf16[32,2,2,256]{3,0,2,1:T(8,128)(2,1)S(1)} %bitcast.219), channel_id=1, replica_groups=mesh['lat'=4,'lon'=32] {'lat'}, dimensions={0}, use_global_device_ids=true | all-gather | bytes 327680 | tf_op jit(solution)/shard_map/all_gather | solution.py:116
  150.4 19.4 %all_to_all.126 = bf16[1,64,4,256]{3,2,0,1:T(4,128)(2,1)S(1)} all-to-all(bf16[1,64,4,256]{3,2,0,1:T(4,128)(2,1)S(1)} %copy.198), channel_id=1, replica_groups=mesh['lat'=4,'lon'=32] {'lon'}, dimensions={1} | all-to-all | bytes 262144 | tf_op jit(solution)/shard_map/all_to_all | solution.py:76
  170.5 10.1 %copy.201 = bf16[1,2,1440,256]{3,1,0,2:T(2,128)(2,1)} copy(bf16[1,2,1440,256]{3,2,1,0:T(8,128)(2,1)S(1)} %fusion.18) | data formatting | bytes 2949120 | tf_op jit(solution)/shard_map/convert_element_type | solution.py:148
  180.6 4.7 %all-to-all-start.3 = ((bf16[1,2,1440,256]{3,1,0,2:T(2,128)(2,1)}), bf16[1,2,1440,256]{3,1,0,2:T(2,128)(2,1)}, u32[]{:S(2)}, u32[]{:S(2)}) async-start(bf16[1,2,1440,256]{3,1,0,2:T(2,128)(2,1)} %copy.201), calls=%async_computation.4 | async-start | bytes 2949120 | tf_op jit(solution)/shard_map/all_to_all | solution.py:72
  192.4 7.5 %fusion.128 = f32[2880,1024]{1,0:T(8,128)} fusion(bf16[2880,256]{1,0:T(8,128)(2,1)} %reshape.401, bf16[1024,256]{1,0:T(8,128)(2,1)S(1)} %copy-done), kind=kOutput, calls=%fused_computation.203 | convolution fusion | flops 1509949440 | bytes 13795328 | tf_op jit(solution)/shard_map/dot_general | solution.py:156
  199.9 7.0 %all-to-all-done.3 = bf16[1,2,1440,256]{3,1,0,2:T(2,128)(2,1)} async-done(((bf16[1,2,1440,256]{3,1,0,2:T(2,128)(2,1)}), bf16[1,2,1440,256]{3,1,0,2:T(2,128)(2,1)}, u32[]{:S(2)}, u32[]{:S(2)}) %all-to-all-start.3) | async-done | bytes 1474592 | tf_op jit(solution)/shard_map/all_to_all | solution.py:72
  213.2 12.6 %fusion.11 = bf16[2880,256]{1,0:T(8,128)(2,1)} fusion(bf16[256,1024]{1,0:T(8,128)(2,1)S(1)} %copy-done.7, f32[2880,1024]{1,0:T(8,128)} %fusion.128, bf16[2880,256]{1,0:T(8,128)(2,1)} %reshape_squeeze.3), kind=kOutput, calls=%fused_computation.16 | convolution fusion | flops 3079618560 | bytes 15269888 | tf_op jit(solution)/shard_map/dot_general | solution.py:162
  229.2 29.2 %all_to_all.127 = bf16[1,64,45,256]{3,2,0,1:T(8,128)(2,1)S(1)} all-to-all(bf16[1,64,45,256]{3,2,0,1:T(8,128)(2,1)} %bitcast.197), channel_id=1, replica_groups=mesh['lat'=4,'lon'=32] {'lon'}, dimensions={1} | all-to-all | bytes 2949120 | tf_op jit(solution)/shard_map/all_to_all | solution.py:76
  260.1 14.1 %all_to_all.128 = bf16[1,2,128,256]{3,1,0,2:T(2,128)(2,1)S(1)} all-to-all(bf16[1,2,128,256]{3,1,0,2:T(2,128)(2,1)S(1)} %copy.207), channel_id=1, replica_groups=mesh['lat'=4,'lon'=32] {'lon'}, dimensions={2} | all-to-all | bytes 262144 | tf_op jit(solution)/shard_map/all_to_all | solution.py:72
  276.1 12.6 %reduce-scatter.5.cloned.1.call-done = bf16[32,2,2,256]{3,0,2,1:T(8,128)(2,1)} async-done(((bf16[128,2,2,256]{3,0,2,1:T(8,128)(2,1)}), bf16[32,2,2,256]{3,0,2,1:T(8,128)(2,1)}) %reduce-scatter.5.cloned.1.call-update) | async-done | bytes 65552 | tf_op jit(solution)/shard_map/reduce_scatter | solution.py:92
  294.6 5.9 %all_gather.7 = bf16[128,2,2,256]{3,0,2,1:T(8,128)(2,1)S(1)} all-gather(bf16[32,2,2,256]{3,0,2,1:T(8,128)(2,1)S(1)} %bitcast.220), channel_id=1, replica_groups=mesh['lat'=4,'lon'=32] {'lat'}, dimensions={0}, use_global_device_ids=true | all-gather | bytes 327680 | tf_op jit(solution)/shard_map/all_gather | solution.py:116
  301.8 20.4 %all_to_all.129 = bf16[2,64,4,256]{3,2,0,1:T(4,128)(2,1)S(1)} all-to-all(bf16[2,64,4,256]{3,2,0,1:T(4,128)(2,1)S(1)} %copy.213), channel_id=1, replica_groups=mesh['lat'=4,'lon'=32] {'lon'}, dimensions={1} | all-to-all | bytes 524288 | tf_op jit(solution)/shard_map/all_to_all | solution.py:76
  323.3 11.6 %copy.216 = bf16[2,2,1440,256]{3,1,0,2:T(2,128)(2,1)S(1)} copy(bf16[2,2,1440,256]{3,2,1,0:T(8,128)(2,1)S(1)} %fusion.14) | data formatting | bytes 5898240 | tf_op jit(solution)/shard_map/convert_element_type | solution.py:191
  334.9 41.4 %all_to_all.130 = bf16[2,2,1440,256]{3,1,0,2:T(2,128)(2,1)S(1)} all-to-all(bf16[2,2,1440,256]{3,1,0,2:T(2,128)(2,1)S(1)} %copy.216), channel_id=1, replica_groups=mesh['lat'=4,'lon'=32] {'lon'}, dimensions={2} | all-to-all | bytes 5898240 | tf_op jit(solution)/shard_map/all_to_all | solution.py:72
  394.0 6.1 %copy.219 = f32[1,32,2,45,256]{4,2,1,3,0:T(2,128)} copy(f32[1,32,2,45,256]{4,1,3,2,0:T(8,128)} %get-tuple-element.20) | data formatting | bytes 5898240 | tf_op jit(solution)/shard_map/convert_element_type | solution.py:195
  400.0 5.1 %reshape.413 = f32[64,45,256]{2,0,1:T(8,128)} reshape(f32[1,32,2,45,256]{4,2,1,3,0:T(2,128)} %copy.219) | data formatting | bytes 5898240 | tf_op jit(solution)/shard_map/convert_element_type | solution.py:195
  405.2 14.0 %collective-permute-done.1 = bf16[64,45,256]{2,0,1:T(8,128)(2,1)} collective-permute-done((bf16[64,45,256]{2,0,1:T(8,128)(2,1)}, bf16[64,45,256]{2,0,1:T(8,128)(2,1)}, u32[]{:S(2)}, u32[]{:S(2)}) %collective-permute-start.1) | collective-permute-done | bytes 1474592 | tf_op jit(solution)/shard_map/ppermute | solution.py:14
  (116 shorter events, 75.8 us)
Async XLA Ops:
  7.2 185.2 %copy-start = (bf16[1024,256]{1,0:T(8,128)(2,1)S(1)}, bf16[1024,256]{1,0:T(8,128)(2,1)}, u32[]{:S(2)}) copy-start(bf16[1024,256]{1,0:T(8,128)(2,1)} %param.12) | copy-start | bytes 1572868
  7.2 35.7 %collective-permute-start = (bf16[64,45,256]{2,0,1:T(8,128)(2,1)}, bf16[64,45,256]{2,0,1:T(8,128)(2,1)S(1)}, u32[]{:S(2)}, u32[]{:S(2)}) collective-permute-start(bf16[64,45,256]{2,0,1:T(8,128)(2,1)} %param.8), channel_id=1, source_target_pairs={{0,16},{1,17},{2,18},{3,19},{4,20},{5,21},{6,22},{7,23},{8,24},{9,... | collective-permute-start | bytes 4423688 | tf_op jit(solution)/shard_map/ppermute | solution.py:14
  49.2 50.1 %all-to-all-start = ((bf16[2,64,45,256]{3,0,2,1:T(2,128)(2,1)}), bf16[2,64,45,256]{3,0,2,1:T(2,128)(2,1)}, u32[]{:S(2)}, u32[]{:S(2)}) async-start(bf16[2,64,45,256]{3,0,2,1:T(2,128)(2,1)} %copy.187), calls=%async_computation | async-start | bytes 5898240 | tf_op jit(solution)/shard_map/all_to_all | solution.py:76
  105.0 17.1 %all-to-all-start.1 = ((bf16[2,2,128,256]{3,1,0,2:T(2,128)(2,1)}), bf16[2,2,128,256]{3,1,0,2:T(2,128)(2,1)S(1)}, u32[]{:S(2)}, u32[]{:S(2)}) async-start(bf16[2,2,128,256]{3,1,0,2:T(2,128)(2,1)} %copy.191), calls=%async_computation.1 | async-start | bytes 524288 | tf_op jit(solution)/shard_map/all_to_all | solution.py:72
  111.3 26.0 %reduce-scatter.3.cloned.1.call-start = ((), (), s32[]{:S(2)}) async-start(), calls=%async_computation.10 | async-start | bytes 327680 | tf_op jit(solution)/shard_map/reduce_scatter | solution.py:92
  122.2 2.1 copy-start.8
  122.4 2.0 copy-start.9
  124.4 17.8 %copy-start.3 = (s32[32]{0:T(128)}, s32[32]{0:T(128)S(1)}, u32[]{:S(2)}) copy-start(s32[32]{0:T(128)S(1)} %compare_select_fusion) | copy-start | bytes 388
  124.4 17.5 %copy-start.5 = (pred[32]{0:T(512)(128)(4,1)}, pred[32]{0:T(512)(128)(4,1)S(1)}, u32[]{:S(2)}) copy-start(pred[32]{0:T(512)(128)(4,1)S(1)} %compare_and_fusion) | copy-start | bytes 100
  180.6 26.2 %all-to-all-start.3 = ((bf16[1,2,1440,256]{3,1,0,2:T(2,128)(2,1)}), bf16[1,2,1440,256]{3,1,0,2:T(2,128)(2,1)}, u32[]{:S(2)}, u32[]{:S(2)}) async-start(bf16[1,2,1440,256]{3,1,0,2:T(2,128)(2,1)} %copy.201), calls=%async_computation.4 | async-start | bytes 2949120 | tf_op jit(solution)/shard_map/all_to_all | solution.py:72
  185.3 103.4 %reduce-scatter.5.cloned.1.call-start = ((), (), s32[]{:S(2)}) async-start(), calls=%async_computation.11 | async-start | bytes 327680 | tf_op jit(solution)/shard_map/reduce_scatter | solution.py:92
  209.8 3.5 copy-start.7
  274.3 16.1 %copy-start.6 = (pred[32]{0:T(512)(128)(4,1)S(1)}, pred[32]{0:T(512)(128)(4,1)}, u32[]{:S(2)}) copy-start(pred[32]{0:T(512)(128)(4,1)} %copy-done.5) | copy-start | bytes 100
  290.6 2.4 copy-start.4
  386.0 33.1 %collective-permute-start.1 = (bf16[64,45,256]{2,0,1:T(8,128)(2,1)}, bf16[64,45,256]{2,0,1:T(8,128)(2,1)}, u32[]{:S(2)}, u32[]{:S(2)}) collective-permute-start(bf16[64,45,256]{2,0,1:T(8,128)(2,1)} %squeeze.20), channel_id=1, source_target_pairs={{0,16},{1,17},{2,18},{3,19},{4,20},{5,21},{6,22},{7,23},{8,24},{9,... | collective-permute-start | bytes 4423688 | tf_op jit(solution)/shard_map/ppermute | solution.py:14
  400.0 19.1 %copy-start.2 = (bf16[64,45,256]{2,0,1:T(8,128)(2,1)S(1)}, bf16[64,45,256]{2,0,1:T(8,128)(2,1)}, u32[]{:S(2)}) copy-start(bf16[64,45,256]{2,0,1:T(8,128)(2,1)} %param.9) | copy-start | bytes 4423684
  400.0 23.2 %copy-start.1 = (bf16[1024,256]{1,0:T(8,128)(2,1)S(1)}, bf16[1024,256]{1,0:T(8,128)(2,1)}, u32[]{:S(2)}) copy-start(bf16[1024,256]{1,0:T(8,128)(2,1)} %param.12) | copy-start | bytes 1572868
Sparse Core Ops, SparseCore 0:
  124.5 12.7 reduce-scatter.2
  276.2 12.4 reduce-scatter.4
where the time goes:
time: 439 us; the launch traced here: 431 us
  blocking collectives  136 us (31%)
  waiting for transfers between devices  124 us (28%)
  local copies, waits for them, and re-layouts  81.5 us (19%)
  starting transfers between devices  27.8 us (6%)
  matrix products  26.2 us (6%)
  other arithmetic  19.9 us (5%)
  between operations  15.1 us (3%)
    all_to_all x3, blocking collectives, transposed(): lax.all_to_all(grid_point_values, 'lon', split_axis=1, concat_axis=2, til...  69 us
    all_to_all x2, blocking collectives, regather(): lax.all_to_all(tile_row_slice, 'lon', split_axis=2, concat_axis=1, tiled=...  55.6 us
    ppermute x2, waiting for transfers between devices, from_partner(): lax.ppermute(value, axis, [(i, i ^ 1 << bit) for i in range(lax.axis_size...  46.5 us
    all_to_all x1, waiting for transfers between devices, transposed(): lax.all_to_all(grid_point_values, 'lon', split_axis=1, concat_axis=2, til...  36.6 us
    reduce_scatter x2, waiting for transfers between devices, lat_section(): lax.psum_scatter(lat_analysis_term(spectrum, cos_tab, sin_tab).astype(jnp...  25.5 us
    all_to_all x2, waiting for transfers between devices, regather(): lax.all_to_all(tile_row_slice, 'lon', split_axis=2, concat_axis=1, tiled=...  15.1 us
    dot_general x1, matrix products, body(): jnp.dot(pre_grad, inner_weight.T, preferred_element_type=jnp.float32)  12.6 us
    all_gather x2, blocking collectives, synthesize(): portion = lax.all_gather(placed, 'lat', axis=0, tiled=True)  11.8 us
  transfers between devices with their start and end apart: 7, of which 7 were waited for; matrix products, arithmetic and copies ran while one was open for 8% of the time, Pallas kernels for 0%

commit v1 on v0

v1 whole, which is shorter than its diff:
```python
import functools
import math

import jax
import jax.numpy as jnp
from jax import lax
from jax.experimental import pallas as pl
from jax.experimental.pallas import tpu as pltpu
from jax.sharding import PartitionSpec as P

BS = 16
KM = 64
KLAT = 128
RING = 4
STEPS = (2, 1, 3)
ROWS, LONS, CH, HID = 64, 45, 256, 1024
LONS_PAD = 48
LON_BLOCKS = 32
KEEP = 32
PIECES = ((48, "xyz"), (48, "yzx"), (32, "zxy"))
MESH = pl.DeviceIdType.MESH
F32, BF16 = jnp.float32, jnp.bfloat16
VMEM = pl.BlockSpec(memory_space=pltpu.VMEM)
LIMIT = 56 << 20
ROW_SPECTRA = [pltpu.VMEM((8192, 128), F32)] * 2


def matmul(a, b, contract=(1, 0)):
    dims = (((contract[0],), (contract[1],)), ((), ()))
    return lax.dot_general(a, b, dims, preferred_element_type=F32)


def own_place():
    lat, lon = lax.axis_index("lat"), lax.axis_index("lon")
    return {
        "x": lax.div(lon, 8),
        "y": lax.rem(lon, 4),
        "z": lax.rem(lax.div(lon, 4), 2) * 2 + lax.div(lat, 2),
        "core": lax.rem(lat, 2),
    }


def moved(at, axis, step):
    return {**at, axis: lax.rem(at[axis] + step, 2 if axis == "core" else RING)}


def device_of(at):
    return (lax.rem(at["z"], 2) * 2 + at["core"], at["x"] * 8 + lax.div(at["z"], 2) * 4 + at["y"])


def greet(at):
    partners = [moved(at, axis, step) for axis in "xyz" for step in STEPS] + [moved(at, "core", 1)]
    barrier = pltpu.get_barrier_semaphore()
    for partner in partners:
        pl.semaphore_signal(barrier, inc=1, device_id=device_of(partner), device_id_type=MESH)
    pl.semaphore_wait(barrier, len(partners))


def send(src, dst, sems, target):
    copy = pltpu.make_async_remote_copy(
        src_ref=src,
        dst_ref=dst,
        send_sem=sems[0],
        recv_sem=sems[1],
        device_id=device_of(target),
        device_id_type=MESH,
    )
    copy.start()
    return copy


def rows(start, size):
    return pl.ds(pl.multiple_of(start, math.gcd(size, 16)), size)


def gather_scratch(pieces):
    n = len(pieces)
    dma = pltpu.SemaphoreType.DMA
    return [dma((n, 3, 3)), dma((n, 3, 3)), dma((n, 4)), dma((n, 4))]


def gather(at, pieces, full, sems):
    ring_send, ring_recv, core_send, core_recv = sems
    bases = [at["core"] * (64 * size) for size, _ in pieces]
    pending = []
    sent = [None] * len(pieces)
    for phase in range(3):
        for i, (size, order) in enumerate(pieces):
            if sent[i]:
                for copy in sent[i]:
                    copy.wait_recv()
            axis = order[2 - phase]
            block = size * RING**phase
            index = 0
            for name in order[: 3 - phase]:
                index = index * RING + at[name]
            here = full[i].at[rows(bases[i] + index * block, block)]
            sent[i] = [
                send(
                    here,
                    here,
                    (ring_send.at[i, phase, s], ring_recv.at[i, phase, s]),
                    moved(at, axis, step),
                )
                for s, step in enumerate(STEPS)
            ]
            pending += sent[i]
    sibling = moved(at, "core", 1)
    across = []
    for s in range(4):
        for i, (size, order) in enumerate(pieces):
            if s:
                sent[i][(1, 2, 0)[s - 1]].wait_recv()
            step = (0, 3, 1, 2)[s]
            slab = lax.rem(at[order[0]] + step, RING)
            here = full[i].at[rows(bases[i] + slab * (16 * size), 16 * size)]
            across.append(send(here, here, (core_send.at[i, s], core_recv.at[i, s]), sibling))
    for copy in across:
        copy.wait_recv()
    for copy in pending + across:
        copy.wait_send()


def scatter_scratch():
    dma = pltpu.SemaphoreType.DMA
    scratch = [dma((3, 3, 3)), dma((3, 3, 3)), dma((3, 4)), dma((3, 4))]
    for size, _ in PIECES:
        scratch += [
            pltpu.VMEM((64 * size, 128), BF16),
            pltpu.VMEM((64 * size, 128), BF16),
            pltpu.VMEM((3, 16 * size, 128), BF16),
            pltpu.VMEM((16 * size, 128), BF16),
            pltpu.VMEM((3, 4 * size, 128), BF16),
            pltpu.VMEM((4 * size, 128), BF16),
            pltpu.VMEM((3, size, 128), BF16),
        ]
    return scratch


def reduce_scatter(at, parts, out, scratch):
    ring_send, ring_recv, core_send, core_recv = scratch[:4]
    bufs = [scratch[4 + 7 * i : 11 + 7 * i] for i in range(3)]
    sibling = moved(at, "core", 1)
    pending, across = [], {}
    for s, step in enumerate(STEPS + (0,)):
        for i, (size, order) in enumerate(PIECES):
            slab = lax.rem(at[order[0]] + step, RING) * (16 * size)
            across[s, i] = send(
                parts[i].at[rows((1 - at["core"]) * (64 * size) + slab, 16 * size)],
                bufs[i][0].at[rows(slab, 16 * size)],
                (core_send.at[i, s], core_recv.at[i, s]),
                sibling,
            )
    sent = [[], [], []]
    for s, step in enumerate(STEPS + (0,)):
        for i, (size, order) in enumerate(PIECES):
            slab = lax.rem(at[order[0]] + step, RING) * (16 * size)
            across[s, i].wait_recv()
            here = rows(slab, 16 * size)
            own = parts[i][rows(at["core"] * (64 * size) + slab, 16 * size), :]
            bufs[i][1][here, :] = (own.astype(F32) + bufs[i][0][here, :].astype(F32)).astype(BF16)
            if step:
                sent[i].append(
                    send(
                        bufs[i][1].at[here],
                        bufs[i][2].at[s],
                        (ring_send.at[i, 0, s], ring_recv.at[i, 0, s]),
                        moved(at, order[0], step),
                    )
                )
    for phase in range(3):
        for i, (size, order) in enumerate(PIECES):
            block = size * RING ** (2 - phase)
            mine, landed = bufs[i][1 + 2 * phase], bufs[i][2 + 2 * phase]
            total = mine[rows(at[order[phase]] * block, block), :].astype(F32)
            for s, copy in enumerate(sent[i]):
                copy.wait_recv()
                total = total + landed[s].astype(F32)
            pending += sent[i]
            if phase == 2:
                if i < 2:
                    out[0:48, 128 * i : 128 * i + 128] = total
                else:
                    out[48:64, 0:128] = total[0:16]
                    out[48:64, 128:256] = total[16:32]
                continue
            after = bufs[i][3 + 2 * phase]
            after[...] = total.astype(BF16)
            small = block // RING
            axis = order[phase + 1]
            sent[i] = [
                send(
                    after.at[rows(lax.rem(at[axis] + step, RING) * small, small)],
                    bufs[i][4 + 2 * phase].at[s],
                    (ring_send.at[i, phase + 1, s], ring_recv.at[i, phase + 1, s]),
                    moved(at, axis, step),
                )
                for s, step in enumerate(STEPS)
            ]
    for copy in pending + list(across.values()):
        copy.wait_send()


def piece_shapes():
    return [jax.ShapeDtypeStruct((128 * size, 128), BF16) for size, _ in PIECES]


def scatter_kernel(px, py, pz, out, *scratch):
    at = own_place()
    greet(at)
    reduce_scatter(at, (px, py, pz), out, scratch)


def scatter_call(parts):
    return pl.pallas_call(
        scatter_kernel,
        out_shape=jax.ShapeDtypeStruct((64, CH), F32),
        in_specs=[VMEM] * 3,
        out_specs=VMEM,
        scratch_shapes=scatter_scratch(),
        compiler_params=pltpu.CompilerParams(
            collective_id=0, has_side_effects=True, vmem_limit_bytes=LIMIT
        ),
        name="reduce_scatter",
    )(*parts)


def own_rows(at, size, order):
    index = 0
    for name in order:
        index = index * RING + at[name]
    return rows((at["core"] * 64 + index) * size, size)


def put_own(at, modes, full):
    for i, (size, order) in enumerate(PIECES):
        if i < 2:
            full[i][own_rows(at, size, order), :] = modes[0:48, 128 * i : 128 * i + 128]
        else:
            both = jnp.concatenate([modes[48:64, 0:128], modes[48:64, 128:256]], axis=0)
            full[i][own_rows(at, size, order), :] = both


def gather_kernel(modes, fx, fy, fz, *sems):
    at = own_place()
    put_own(at, modes, (fx, fy, fz))
    greet(at)
    gather(at, PIECES, (fx, fy, fz), sems)


def gather_call(modes):
    return pl.pallas_call(
        gather_kernel,
        out_shape=piece_shapes(),
        in_specs=[VMEM],
        out_specs=[VMEM] * 3,
        scratch_shapes=gather_scratch(PIECES),
        compiler_params=pltpu.CompilerParams(
            collective_id=1, has_side_effects=True, vmem_limit_bytes=LIMIT
        ),
        name="all_gather",
    )(modes)


KEPT_PIECE = ((8, "xyz"),)


def kept_kernel(kept, full, *sems):
    at = own_place()
    full[pl.ds(pl.multiple_of((at["core"] * 64 + (at["x"] * 4 + at["y"]) * 4 + at["z"]) * 8, 8), 8), :] = (
        jnp.broadcast_to(kept[...], (8, 128))
    )
    greet(at)
    gather(at, KEPT_PIECE, (full,), sems)


def kept_call(kept):
    return pl.pallas_call(
        kept_kernel,
        out_shape=jax.ShapeDtypeStruct((1024, 128), jnp.int32),
        in_specs=[VMEM],
        out_specs=VMEM,
        scratch_shapes=gather_scratch(KEPT_PIECE),
        compiler_params=pltpu.CompilerParams(collective_id=2, has_side_effects=True),
        name="gather_kept",
    )(kept)


def split_block(b):
    return {"x": lax.div(b, 8), "zhi": lax.rem(lax.div(b, 4), 2), "y": lax.rem(b, 4)}


def piece_start(b, lat, size, order):
    place = split_block(b)
    place["z"] = place["zhi"] * 2 + lat // 2
    index = 0
    for name in order:
        index = index * RING + place[name]
    return rows((lat % 2 * 64 + index) * size, size)


def one_hot(slots, b):
    ids = lax.broadcasted_iota(jnp.int32, (256, 128), 0)
    return jnp.where(ids == slots[pl.ds(b, 1), :], 1.0, 0.0).astype(BF16)


def put_row(halves, g, value):
    for i, half in enumerate(halves):
        half[pl.ds(g, 128, stride=ROWS), :] = value[:, 128 * i : 128 * i + 128]


def get_row(halves, g):
    return jnp.concatenate([half[pl.ds(g, 128, stride=ROWS), :] for half in halves], axis=1)


def put_block(halves, start, value):
    for i, half in enumerate(halves):
        half[pl.ds(start, 128), :] = value[:, 128 * i : 128 * i + 128]


def get_block(halves, start):
    return jnp.concatenate([half[pl.ds(start, 128), :] for half in halves], axis=1)


def analyse_latitude(rows_spec, slots, table, parts):
    def block(b, carry):
        start = pl.multiple_of(b * 256, 256)
        hot = one_hot(slots, b)
        dense = [
            matmul(table[mode], get_block(rows_spec, start + 128 * mode).astype(BF16)).astype(BF16)
            for mode in range(2)
        ]
        for part in range(2):
            both = jnp.concatenate([d[128 * part : 128 * part + 128] for d in dense], axis=0)
            modes = matmul(hot, both, (0, 0)).astype(BF16)
            for lat in range(4):
                tile = modes[32 * lat : 32 * lat + 32]
                px = parts[0].at[piece_start(b, lat, 48, "xyz")]
                py = parts[1].at[piece_start(b, lat, 48, "yzx")]
                pz = parts[2].at[piece_start(b, lat, 32, "zxy")]
                if part == 0:
                    px[0:32, :] = tile[:, 0:128]
                    py[0:32, :] = tile[:, 128:256]
                else:
                    px[32:48, :] = tile[0:16, 0:128]
                    py[32:48, :] = tile[0:16, 128:256]
                    pz[0:16, :] = tile[16:32, 0:128]
                    pz[16:32, :] = tile[16:32, 128:256]
        return carry

    lax.fori_loop(0, LON_BLOCKS, block, 0)


def synthesise_latitude(full, slots, table, rows_spec):
    def block(b, carry):
        start = pl.multiple_of(b * 256, 256)
        hot = one_hot(slots, b)
        tiles = [[], []]
        for lat in range(4):
            px = full[0][piece_start(b, lat, 48, "xyz"), :]
            py = full[1][piece_start(b, lat, 48, "yzx"), :]
            pz = full[2][piece_start(b, lat, 32, "zxy"), :]
            tiles[0].append(jnp.concatenate([px[0:32], py[0:32]], axis=1))
            tiles[1].append(
                jnp.concatenate(
                    [
                        jnp.concatenate([px[32:48], py[32:48]], axis=1),
                        jnp.concatenate([pz[0:16], pz[16:32]], axis=1),
                    ],
                    axis=0,
                )
            )
        placed = [
            matmul(hot, jnp.concatenate(tiles[part], axis=0)).astype(BF16) for part in range(2)
        ]
        for mode in range(2):
            both = jnp.concatenate([p[128 * mode : 128 * mode + 128] for p in placed], axis=0)
            put_block(rows_spec, start + 128 * mode, matmul(table[mode], both))
        return carry

    lax.fori_loop(0, LON_BLOCKS, block, 0)


def forward_kernel(field, slots, table, basis, px, py, pz, *rows_spec):
    def row(g, carry):
        put_row(rows_spec, g, matmul(basis[:, 0:LONS], field[g]))
        return carry

    lax.fori_loop(0, ROWS, row, 0)
    analyse_latitude(rows_spec, slots, table, (px, py, pz))


def forward_call(field, slots, table, basis):
    return pl.pallas_call(
        forward_kernel,
        out_shape=piece_shapes(),
        in_specs=[VMEM] * 4,
        out_specs=[VMEM] * 3,
        scratch_shapes=ROW_SPECTRA,
        compiler_params=pltpu.CompilerParams(vmem_limit_bytes=LIMIT),
        name="forward",
    )(field, slots, table, basis)


def gelu_slope(x):
    c, a = math.sqrt(2.0 / math.pi), 0.044715
    square = x * x
    t = jnp.tanh(x * (c + (c * a) * square))
    half = 0.5 + 0.5 * t
    return half + x * (half * (1.0 - t)) * (c + (3.0 * c * a) * square)


GROUP = 8


def middle_kernel(
    fx, fy, fz, out_grad, slots, table, table_back, basis, basis_back, w1, w2, px, py, pz, grads, grid, *rows_spec
):
    grads[:, LONS:LONS_PAD, :] = jnp.zeros((ROWS, LONS_PAD - LONS, CH), BF16)
    grads[:, 0:LONS, :] = out_grad[...]
    synthesise_latitude((fx, fy, fz), slots, table_back, rows_spec)

    def row(g, carry):
        spec = get_row(rows_spec, g).astype(BF16)
        grid[g] = matmul(basis_back[...], spec).astype(BF16)
        return carry

    lax.fori_loop(0, ROWS, row, 0)

    def points(i, carry):
        here = pl.ds(i * GROUP, GROUP)
        value = grid[here].reshape(GROUP * LONS_PAD, CH)
        grad = grads[here].reshape(GROUP * LONS_PAD, CH)
        total = jnp.zeros((GROUP * LONS_PAD, CH), F32)
        for k in range(HID // 256):
            cols = slice(256 * k, 256 * k + 256)
            pre = matmul(value, w1[:, cols])
            hidden = matmul(grad, w2[cols, :], (1, 1))
            pre_grad = (gelu_slope(pre) * hidden).astype(BF16)
            total = total + matmul(pre_grad, w1[:, cols], (1, 1))
        grid[here] = total.astype(BF16).reshape(GROUP, LONS_PAD, CH)
        return carry

    lax.fori_loop(0, ROWS // GROUP, points, 0)

    def back(g, carry):
        put_row(rows_spec, g, matmul(basis[...], grid[g]))
        return carry

    lax.fori_loop(0, ROWS, back, 0)
    analyse_latitude(rows_spec, slots, table, (px, py, pz))


def middle_call(full, out_grad, slots, table, table_back, basis, basis_back, w1, w2):
    return pl.pallas_call(
        middle_kernel,
        out_shape=piece_shapes(),
        in_specs=[VMEM] * 11,
        out_specs=[VMEM] * 3,
        scratch_shapes=[
            pltpu.VMEM((ROWS, LONS_PAD, CH), BF16),
            pltpu.VMEM((ROWS, LONS_PAD, CH), BF16),
            *ROW_SPECTRA,
        ],
        compiler_params=pltpu.CompilerParams(vmem_limit_bytes=LIMIT),
        name="middle",
    )(*full, out_grad, slots, table, table_back, basis, basis_back, w1, w2)


def last_kernel(scale, fx, fy, fz, out_grad, slots, table_back, basis_back, out, *rows_spec):
    synthesise_latitude((fx, fy, fz), slots, table_back, rows_spec)

    def row(g, carry):
        spec = get_row(rows_spec, g).astype(BF16)
        part = (matmul(basis_back[...], spec) * scale)[0:LONS]
        out[g] = (out_grad[g].astype(F32) + part).astype(BF16)
        return carry

    lax.fori_loop(0, ROWS, row, 0)


def last_call(scale, full, out_grad, slots, table_back, basis_back):
    return pl.pallas_call(
        functools.partial(last_kernel, scale),
        out_shape=jax.ShapeDtypeStruct((ROWS, LONS, CH), BF16),
        in_specs=[VMEM] * 7,
        out_specs=VMEM,
        scratch_shapes=ROW_SPECTRA,
        compiler_params=pltpu.CompilerParams(vmem_limit_bytes=LIMIT),
        name="last",
    )(*full, out_grad, slots, table_back, basis_back)


def longitude_tables(lon_rank, lon_total):
    lon_ids = lon_rank * LONS + jnp.arange(LONS_PAD, dtype=jnp.int32)
    q = jnp.arange(2 * KM, dtype=jnp.int32)
    mode, part = q // 2, q % 2
    phases = lon_ids[None, :] * mode[:, None] % lon_total
    angles = phases.astype(F32) * (2.0 * math.pi / lon_total)
    basis = jnp.where(part[:, None] == 0, jnp.cos(angles), -jnp.sin(angles))
    basis = jnp.where(jnp.arange(LONS_PAD)[None, :] < LONS, basis, 0.0).astype(BF16)
    return basis, basis.T


def latitude_tables(row_ids, lat_total):
    wave = jnp.arange(KLAT, dtype=jnp.int32) - KLAT // 2

    def angles(ids):
        phases = jnp.mod(wave[:, None] * ids[None, :], 2 * lat_total)
        return phases.astype(F32) * (math.pi / lat_total)

    upper, lower = angles(row_ids), angles(2 * lat_total - 1 - row_ids)
    cu, su, cl, sl = jnp.cos(upper), jnp.sin(upper), jnp.cos(lower), jnp.sin(lower)

    def table(c, s):
        return jnp.concatenate(
            [jnp.concatenate([c, s], axis=1), jnp.concatenate([-s, c], axis=1)], axis=0
        )

    plain = table(cu, su)
    doubled = jnp.stack([table(cu + cl, su + sl), table(cu - cl, su - sl)])
    return jnp.stack([plain, plain]).astype(BF16), doubled.astype(BF16)


def body(in_field, out_grad, spec_weight, inner_weight, output_projection_weight, kept_modes):
    lat_parts, lon_parts = lax.axis_size("lat"), lax.axis_size("lon")
    lat_total, lon_total = ROWS * lat_parts, LONS * lon_parts
    fwd_scale = 1.0 / math.sqrt(2 * lat_total * lon_total)
    syn_scale = 1.0 / math.sqrt(KEEP * lat_parts * lon_parts)
    highest = lax.Precision.HIGHEST
    lat_rank, lon_rank = lax.axis_index("lat"), lax.axis_index("lon")

    kept = kept_call(jnp.pad(kept_modes, (0, 128 - KEEP)).reshape(1, 128))
    kept = kept.reshape(2, 4, 4, 2, 2, 8, 128)[..., 0, :KEEP]
    kept = jnp.transpose(kept, (1, 3, 2, 4, 0, 5)).reshape(LON_BLOCKS, 4, KEEP)
    lat_base = jnp.arange(4, dtype=jnp.int32)[None, :, None] * 32
    slots = (kept % 2 * KLAT + lat_base + kept // 2).reshape(LON_BLOCKS, 4 * KEEP)

    basis, basis_back = longitude_tables(lon_rank, lon_total)
    plain, doubled = latitude_tables(
        lat_rank * ROWS + jnp.arange(ROWS, dtype=jnp.int32), lat_total
    )
    plain_back, doubled_back = jnp.swapaxes(plain, 1, 2), jnp.swapaxes(doubled, 1, 2)

    modes_in = scatter_call(forward_call(in_field, slots, doubled, basis)) * fwd_scale
    xr, xi = modes_in.reshape(2, KEEP, CH // BS, BS)
    weights = spec_weight.astype(F32).reshape(KEEP, 2, CH // BS, BS, BS)
    wr, wi = weights[:, 0], weights[:, 1]

    def mix(a, b):
        return jnp.einsum("qbi,qbio->qbo", a, b, precision=highest)

    mixed = jnp.stack([mix(xr, wr) - mix(xi, wi), mix(xr, wi) + mix(xi, wr)])
    mixed = mixed.reshape(2 * KEEP, CH).astype(BF16)

    scaled_back = (basis_back.astype(F32) * syn_scale).astype(BF16)
    parts = middle_call(
        gather_call(mixed),
        out_grad,
        slots,
        plain,
        plain_back,
        basis,
        scaled_back,
        inner_weight,
        output_projection_weight,
    )
    modes_grad = scatter_call(parts) * syn_scale
    gr, gi = modes_grad.reshape(2, KEEP, CH // BS, BS)

    def mix_back(a, b):
        return jnp.einsum("qbo,qbio->qbi", a, b, precision=highest)

    back = jnp.stack([mix_back(gr, wr) + mix_back(gi, wi), mix_back(gi, wr) - mix_back(gr, wi)])
    back = back.reshape(2 * KEEP, CH).astype(BF16)
    input_grad = last_call(
        fwd_scale, gather_call(back), out_grad, slots, doubled_back, basis_back
    )

    def outer(a, b):
        return a[:, :, :, None] * b[:, :, None, :]

    spectral_grad = jnp.stack(
        [outer(xr, gr) + outer(xi, gi), outer(xr, gi) - outer(xi, gr)], axis=1
    ).reshape(KEEP, 2, CH // BS, BS * BS)
    return input_grad, spectral_grad


def solution(mesh):
    return jax.shard_map(
        body,
        mesh=mesh,
        in_specs=(
            P("lat", "lon", None),
            P("lat", "lon", None),
            P(("lat", "lon"), None, None, None),
            P(),
            P(),
            P(("lat", "lon")),
        ),
        out_specs=(P("lat", "lon", None), P(("lat", "lon"), None, None, None)),
        check_vma=False,
    )
```

time: 439 us -> 296 us (0.67); the launches traced: 431 us -> 294 us
  Pallas kernels: 0 us -> 262 us
  blocking collectives: 136 us -> 0 us
  waiting for transfers between devices: 124 us -> 0 us
  local copies, waits for them, and re-layouts: 81.5 us -> 19 us
  starting transfers between devices: 27.8 us -> 0 us
  matrix products: 26.2 us -> 0 us
  between operations: 15.1 us -> 0.9 us
  other arithmetic: 19.9 us -> 12.5 us
    pallas_call x0 -> x8, Pallas kernels: none -> 262 us  [the longest x1 72.8 us: middle_call(): pl.pallas_call(middle_kernel, out_shape=piece_shapes(), in_specs=[VMEM] *...]
    all_to_all x5 -> x0, blocking collectives: 125 us -> none  [the longest x3 69 us: transposed(): lax.all_to_all(grid_point_values, 'lon', split_axis=1, concat_axis=2, til...]
    all_to_all x3 -> x0, waiting for transfers between devices: 51.7 us -> none  [the longest x1 36.6 us: transposed(): lax.all_to_all(grid_point_values, 'lon', split_axis=1, concat_axis=2, til...]
    ppermute x2 -> x0, waiting for transfers between devices: 46.5 us -> none  [from_partner(): lax.ppermute(value, axis, [(i, i ^ 1 << bit) for i in range(lax.axis_size...]
    convert_element_type x8 -> x4, local copies, waits for them, and re-layouts: 34.3 us -> 1.64 us  [the longest x2 0.82 us: body(): mixed = mixed.reshape(2 * KEEP, CH).astype(BF16)]
    dot_general x14 -> x0, matrix products: 26.2 us -> none  [the longest x1 12.6 us: body(): jnp.dot(pre_grad, inner_weight.T, preferred_element_type=jnp.float32)]
    reduce_scatter x2 -> x0, waiting for transfers between devices: 25.5 us -> none  [lat_section(): lax.psum_scatter(lat_analysis_term(spectrum, cos_tab, sin_tab).astype(jnp...]
    all_to_all x3 -> x0, starting transfers between devices: 22 us -> none  [the longest x2 11 us: regather(): lax.all_to_all(tile_row_slice, 'lon', split_axis=2, concat_axis=1, tiled=...]
  transfers between devices with their start and end apart: 7 -> 0, of which waited for: 7 -> 0; matrix products, arithmetic and copies ran while one was open for 8% -> 0% of each run, Pallas kernels for 0% -> 0%
where the time goes in v1:
time: 296 us; the launch traced here: 294 us
  Pallas kernels  262 us (89%)
  local copies, waits for them, and re-layouts  19 us (6%)
  other arithmetic  12.5 us (4%)
    pallas_call x1, Pallas kernels, middle_call(): pl.pallas_call(middle_kernel, out_shape=piece_shapes(), in_specs=[VMEM] *...  72.8 us
    pallas_call x2, Pallas kernels, scatter_call(): pl.pallas_call(scatter_kernel, out_shape=jax.ShapeDtypeStruct((64, CH), F...  53.9 us
    pallas_call x2, Pallas kernels, gather_call(): pl.pallas_call(gather_kernel, out_shape=piece_shapes(), in_specs=[VMEM],...  49 us
    pallas_call x1, Pallas kernels, last_call(): pl.pallas_call(functools.partial(last_kernel, scale), out_shape=jax.Shape...  33.4 us
    pallas_call x1, Pallas kernels, forward_call(): pl.pallas_call(forward_kernel, out_shape=piece_shapes(), in_specs=[VMEM]...  32 us
    pallas_call x1, Pallas kernels, kept_call(): pl.pallas_call(kept_kernel, out_shape=jax.ShapeDtypeStruct((1024, 128), j...  20.5 us
    unnamed x9, local copies, waits for them, and re-layouts  9.62 us

profile of v1, /device:TPU:0, one launch (start us, length us, event | category | flops | bytes accessed | tf_op | source)
XLA Modules:
  0.0 294.1 jit_solution(1177653731395855808)
XLA Ops:
  0.7 1.3 pad_bitcast_fusion.kept
  2.1 0.8 select_convert_fusion.1
  2.9 1.0 select_convert_fusion.basis
  5.2 0.8 copy.49.table
  7.4 20.5 %gather_kept.1 = s32[1024,128]{1,0:T(8,128)} custom-call(s32[1,128]{1,0:T(1,128)} %pad_bitcast_fusion.kept), custom_call_target="tpu_custom_call" | custom-call | tf_op jit(solution)/shard_map/gather_kept/pallas_call | solution.py:278
  27.9 1.1 slice.16
  29.8 2.0 copy.55.out_grad
  31.8 3.5 %copy.48.field = bf16[64,45,256]{2,1,0:T(8,128)(2,1)} copy(bf16[64,45,256]{2,0,1:T(8,128)(2,1)} %param.6) | data formatting | bytes 2949120 | tf_op args[0]
  35.3 1.1 copy.51
  36.4 32.0 %forward.1 = (bf16[6144,128]{1,0:T(8,128)(2,1)}, bf16[6144,128]{1,0:T(8,128)(2,1)}, bf16[4096,128]{1,0:T(8,128)(2,1)}) custom-call(bf16[64,45,256]{2,1,0:T(8,128)(2,1)} %copy.48.field, s32[32,128]{1,0:T(8,128)} %fusion.31.slots, bf16[2,256,128]{2,1,0:T(8,128)(2,1)} %copy.49.table, bf16[128,48]{1,0:T(8,128)(2,1)} %select_convert_fusion.basis), custom_call_target="tpu_custom_call" | custom-call | tf_op jit(solution)/shard_map/forward/pallas_call | solution.py:394
  68.4 26.5 %reduce_scatter.2 = f32[64,256]{1,0:T(8,128)} custom-call(bf16[6144,128]{1,0:T(8,128)(2,1)} %get-tuple-element.14.px, bf16[6144,128]{1,0:T(8,128)(2,1)} %get-tuple-element.15.py, bf16[4096,128]{1,0:T(8,128)(2,1)} %get-tuple-element.16.pz), custom_call_target="tpu_custom_call" | custom-call | tf_op jit(solution)/shard_map/reduce_scatter/pallas_call | solution.py:215
  94.9 0.8 broadcast_multiply_fusion.1
  96.0 1.1 fusion.2
  98.1 24.4 %all_gather.2 = (bf16[6144,128]{1,0:T(8,128)(2,1)}, bf16[6144,128]{1,0:T(8,128)(2,1)}, bf16[4096,128]{1,0:T(8,128)(2,1)}) custom-call(bf16[64,256]{1,0:T(8,128)(2,1)} %copy.54.modes), custom_call_target="tpu_custom_call" | custom-call | tf_op jit(solution)/shard_map/all_gather/pallas_call | solution.py:252
  122.5 72.8 %middle.1 = (bf16[6144,128]{1,0:T(8,128)(2,1)}, bf16[6144,128]{1,0:T(8,128)(2,1)}, bf16[4096,128]{1,0:T(8,128)(2,1)}) custom-call(bf16[6144,128]{1,0:T(8,128)(2,1)} %get-tuple-element.17.fx, bf16[6144,128]{1,0:T(8,128)(2,1)} %get-tuple-element.18.fy, bf16[4096,128]{1,0:T(8,128)(2,1)} %get-tuple-element.19.fz, bf16[64,45,256]{2,1,0:T(8,128)(2,1)} %copy.55.out_grad, ...), custom_call_target="tpu_custom_call" | custom-call | tf_op jit(solution)/shard_map/middle/pallas_call | solution.py:455
  195.4 27.4 %reduce_scatter.3 = f32[64,256]{1,0:T(8,128)} custom-call(bf16[6144,128]{1,0:T(8,128)(2,1)} %get-tuple-element.20.px, bf16[6144,128]{1,0:T(8,128)(2,1)} %get-tuple-element.21.py, bf16[4096,128]{1,0:T(8,128)(2,1)} %get-tuple-element.22.pz), custom_call_target="tpu_custom_call" | custom-call | tf_op jit(solution)/shard_map/reduce_scatter/pallas_call | solution.py:215
  222.8 0.8 broadcast_multiply_fusion
  223.8 2.2 fusion.6
  227.1 1.9 multiply_add_fusion
  229.0 2.3 copy.62
  232.0 1.1 pad_maximum_fusion
  233.1 24.6 %all_gather.3 = (bf16[6144,128]{1,0:T(8,128)(2,1)}, bf16[6144,128]{1,0:T(8,128)(2,1)}, bf16[4096,128]{1,0:T(8,128)(2,1)}) custom-call(bf16[64,256]{1,0:T(8,128)(2,1)} %copy.60.modes), custom_call_target="tpu_custom_call" | custom-call | tf_op jit(solution)/shard_map/all_gather/pallas_call | solution.py:252
  257.7 33.4 %last.1 = bf16[64,45,256]{2,1,0:T(8,128)(2,1)} custom-call(bf16[6144,128]{1,0:T(8,128)(2,1)} %get-tuple-element.23.fx, bf16[6144,128]{1,0:T(8,128)(2,1)} %get-tuple-element.24.fy, bf16[4096,128]{1,0:T(8,128)(2,1)} %get-tuple-element.25.fz, bf16[64,45,256]{2,1,0:T(8,128)(2,1)} %copy.55.out_grad, s32[32,128]{1,0:T(8,128)} %fusion.31.slots, ...), custom_call_target="tpu_custom_call" | custom-call | tf_op jit(solution)/shard_map/last/pallas_call | solution.py:483
  291.0 3.0 %copy.64 = bf16[64,45,256]{2,0,1:T(8,128)(2,1)} copy(bf16[64,45,256]{2,1,0:T(8,128)(2,1)} %last.1) | data formatting | bytes 2949120
  (43 shorter events, 6.8 us)
Async XLA Ops:
  0.6 29.2 %copy-start = (bf16[64,45,256]{2,0,1:T(8,128)(2,1)S(1)}, bf16[64,45,256]{2,0,1:T(8,128)(2,1)}, u32[]{:S(2)}) copy-start(bf16[64,45,256]{2,0,1:T(8,128)(2,1)} %param.7) | copy-start | bytes 4423684
  31.8 3.5 %copy-start.1 = (bf16[32,2,16,256]{3,2,1,0:T(8,128)(2,1)S(1)}, bf16[32,2,16,256]{3,2,1,0:T(8,128)(2,1)}, u32[]{:S(2)}) copy-start(bf16[32,2,16,256]{3,2,1,0:T(8,128)(2,1)} %param.8) | copy-start | bytes 1572868

commit v2 on v1

v2 whole, which is shorter than its diff:
```python
import functools
import math

import jax
import jax.numpy as jnp
import numpy as np
from jax import lax
from jax.experimental import pallas as pl
from jax.experimental.pallas import tpu as pltpu
from jax.sharding import PartitionSpec as P

BS = 16
KM = 64
KLAT = 128
RING = 4
STEPS = (2, 1, 3)
ROWS, LONS, CH, HID = 64, 45, 256, 1024
LONS_PAD = 48
LON_BLOCKS = 32
KEEP = 32
PIECES = ((48, "xyz"), (48, "yzx"), (32, "zxy"))
MESH = pl.DeviceIdType.MESH
F32, BF16 = jnp.float32, jnp.bfloat16
VMEM = pl.BlockSpec(memory_space=pltpu.VMEM)
LIMIT = 60 << 20
U_FILL, U_ROW, U_BLK, GROUP, CHUNK = 5, 16, 8, 9, 256


def matmul(a, b, contract=(1, 0)):
    dims = (((contract[0],), (contract[1],)), ((), ()))
    return lax.dot_general(a, b, dims, preferred_element_type=F32)


def own_place():
    lat, lon = lax.axis_index("lat"), lax.axis_index("lon")
    return {
        "x": lax.div(lon, 8),
        "y": lax.rem(lon, 4),
        "z": lax.rem(lax.div(lon, 4), 2) * 2 + lax.div(lat, 2),
        "core": lax.rem(lat, 2),
    }


def moved(at, axis, step):
    return {**at, axis: lax.rem(at[axis] + step, 2 if axis == "core" else RING)}


def device_of(at):
    return (lax.rem(at["z"], 2) * 2 + at["core"], at["x"] * 8 + lax.div(at["z"], 2) * 4 + at["y"])


def greet(at):
    partners = [moved(at, axis, step) for axis in "xyz" for step in STEPS] + [moved(at, "core", 1)]
    for partner in partners:
        pl.semaphore_signal(
            pltpu.get_barrier_semaphore(),
            inc=1,
            device_id=device_of(partner),
            device_id_type=MESH,
        )
    return len(partners)


def send(src, dst, sems, target):
    copy = pltpu.make_async_remote_copy(
        src_ref=src,
        dst_ref=dst,
        send_sem=sems[0],
        recv_sem=sems[1],
        device_id=device_of(target),
        device_id_type=MESH,
    )
    copy.start()
    return copy


def rows(start, size):
    return pl.ds(pl.multiple_of(start, math.gcd(size, 16)), size)


def index_of(at, order):
    index = 0
    for name in order:
        index = index * RING + at[name]
    return index


def gather_sems(pieces):
    n, dma = len(pieces), pltpu.SemaphoreType.DMA
    return [dma((n, 3, 3)), dma((n, 3, 3)), dma((n, 4)), dma((n, 4))]


def gather(at, pieces, full, sems):
    ring_send, ring_recv, core_send, core_recv = sems
    bases = [at["core"] * (64 * size) for size, _ in pieces]
    sibling = moved(at, "core", 1)
    pending, across = [], []
    sent = [[] for _ in pieces]

    def across_core(i, s, step):
        size, order = pieces[i]
        slab = lax.rem(at[order[0]] + step, RING)
        here = full[i].at[rows(bases[i] + slab * (16 * size), 16 * size)]
        across.append(send(here, here, (core_send.at[i, s], core_recv.at[i, s]), sibling))

    for phase in range(3):
        for i, (size, order) in enumerate(pieces):
            for copy in sent[i]:
                copy.wait_recv()
            block = size * RING**phase
            index = index_of(at, order[: 3 - phase])
            here = full[i].at[rows(bases[i] + index * block, block)]
            sent[i] = [
                send(
                    here,
                    here,
                    (ring_send.at[i, phase, s], ring_recv.at[i, phase, s]),
                    moved(at, order[2 - phase], step),
                )
                for s, step in enumerate(STEPS)
            ]
            pending += sent[i]
            if phase == 2:
                across_core(i, 0, 0)
        yield
    for s in (1, 2, 0):
        for i in range(len(pieces)):
            sent[i][s].wait_recv()
            across_core(i, s + 1, RING - STEPS[s])
    for copy in across:
        copy.wait_recv()
    for copy in pending + across:
        copy.wait_send()


def scatter_scratch():
    dma = pltpu.SemaphoreType.DMA
    scratch = [dma((3, 3, 3)), dma((3, 3, 3)), dma((3, 4)), dma((3, 4))]
    for size, _ in PIECES:
        scratch += [
            pltpu.VMEM((64 * size, 128), BF16),
            pltpu.VMEM((64 * size, 128), BF16),
            pltpu.VMEM((3, 16 * size, 128), BF16),
            pltpu.VMEM((16 * size, 128), BF16),
            pltpu.VMEM((3, 4 * size, 128), BF16),
            pltpu.VMEM((4 * size, 128), BF16),
            pltpu.VMEM((3, size, 128), BF16),
        ]
    return scratch


def reduce_scatter(at, parts, scale, out, scratch):
    ring_send, ring_recv, core_send, core_recv = scratch[:4]
    bufs = [scratch[4 + 7 * i : 11 + 7 * i] for i in range(3)]
    sibling = moved(at, "core", 1)
    pending, across = [], {}
    for s, step in enumerate(STEPS + (0,)):
        for i, (size, order) in enumerate(PIECES):
            slab = lax.rem(at[order[0]] + step, RING) * (16 * size)
            across[s, i] = send(
                parts[i].at[rows((1 - at["core"]) * (64 * size) + slab, 16 * size)],
                bufs[i][0].at[rows(slab, 16 * size)],
                (core_send.at[i, s], core_recv.at[i, s]),
                sibling,
            )
    sent = [[], [], []]
    for s, step in enumerate(STEPS + (0,)):
        for i, (size, order) in enumerate(PIECES):
            slab = lax.rem(at[order[0]] + step, RING) * (16 * size)
            across[s, i].wait_recv()
            here = rows(slab, 16 * size)
            own = parts[i][rows(at["core"] * (64 * size) + slab, 16 * size), :]
            bufs[i][1][here, :] = (own.astype(F32) + bufs[i][0][here, :].astype(F32)).astype(BF16)
            if step:
                sent[i].append(
                    send(
                        bufs[i][1].at[here],
                        bufs[i][2].at[s],
                        (ring_send.at[i, 0, s], ring_recv.at[i, 0, s]),
                        moved(at, order[0], step),
                    )
                )
    yield
    for phase in range(3):
        for i, (size, order) in enumerate(PIECES):
            block = size * RING ** (2 - phase)
            mine, landed = bufs[i][1 + 2 * phase], bufs[i][2 + 2 * phase]
            total = mine[rows(at[order[phase]] * block, block), :].astype(F32)
            for s, copy in enumerate(sent[i]):
                copy.wait_recv()
                total = total + landed[s].astype(F32)
            pending += sent[i]
            if phase == 2:
                total = total * scale
                if i < 2:
                    out[0:48, 128 * i : 128 * i + 128] = total
                else:
                    out[48:64, 0:128] = total[0:16]
                    out[48:64, 128:256] = total[16:32]
                continue
            after = bufs[i][3 + 2 * phase]
            after[...] = total.astype(BF16)
            small = block // RING
            axis = order[phase + 1]
            sent[i] = [
                send(
                    after.at[rows(lax.rem(at[axis] + step, RING) * small, small)],
                    bufs[i][4 + 2 * phase].at[s],
                    (ring_send.at[i, phase + 1, s], ring_recv.at[i, phase + 1, s]),
                    moved(at, axis, step),
                )
                for s, step in enumerate(STEPS)
            ]
        if phase < 2:
            yield
    for copy in pending + list(across.values()):
        copy.wait_send()


def run(steps, *between):
    work = list(between)
    for _ in steps:
        if work:
            work.pop(0)()


def put_own(at, modes, full):
    for i, (size, order) in enumerate(PIECES):
        here = rows((at["core"] * 64 + index_of(at, order)) * size, size)
        if i < 2:
            full[i][here, :] = modes[0:48, 128 * i : 128 * i + 128]
        else:
            full[i][here, :] = jnp.concatenate(
                [modes[48:64, 0:128], modes[48:64, 128:256]], axis=0
            )


def split_block(b):
    return {"x": lax.div(b, 8), "zhi": lax.rem(lax.div(b, 4), 2), "y": lax.rem(b, 4)}


def piece_start(b, lat, size, order):
    place = split_block(b)
    place["z"] = place["zhi"] * 2 + lat // 2
    index = 0
    for name in order:
        index = index * RING + place[name]
    return rows((lat % 2 * 64 + index) * size, size)


def put(halves, where, value):
    for i, half in enumerate(halves):
        half[where, :] = value[:, 128 * i : 128 * i + 128]


def get(halves, where):
    return jnp.concatenate([half[where, :] for half in halves], axis=1)


def one_hot(slots, b):
    ids = lax.broadcasted_iota(jnp.int32, (256, 128), 0).astype(F32)
    return jnp.where(ids == slots[pl.ds(b, 1), :], 1.0, 0.0).astype(BF16)


def one_hot_turned(slots, b):
    columns = jnp.transpose(jnp.broadcast_to(slots[pl.ds(b, 1), :], (128, 128)))
    ids = lax.broadcasted_iota(jnp.int32, (128, 128), 1).astype(F32)
    hot = [jnp.where(ids == columns - 128.0 * mode, 1.0, 0.0).astype(BF16) for mode in range(2)]
    return jnp.concatenate(hot, axis=1)


def fill_points(field, points):
    def one(j, carry):
        put(points, pl.ds(pl.multiple_of(j * ROWS, ROWS), ROWS), field[j].astype(F32))
        return carry

    lax.fori_loop(0, LONS, one, 0, unroll=U_FILL)
    tail = pl.ds(LONS * ROWS, (LONS_PAD - LONS) * ROWS)
    put(points, tail, jnp.zeros(((LONS_PAD - LONS) * ROWS, CH), F32))


def analyse_longitude(points, basis, rows_spec):
    def one(g, carry):
        value = get(points, pl.ds(g, LONS_PAD, stride=ROWS)).astype(BF16)
        put(rows_spec, pl.ds(g, 2 * KM, stride=ROWS), matmul(basis[...], value))
        return carry

    lax.fori_loop(0, ROWS, one, 0, unroll=U_ROW)


def synthesise_longitude(rows_spec, basis_back, points, scale):
    def one(g, carry):
        spec = get(rows_spec, pl.ds(g, 2 * KM, stride=ROWS)).astype(BF16)
        put(points, pl.ds(g, LONS_PAD, stride=ROWS), matmul(basis_back[...], spec) * scale)
        return carry

    lax.fori_loop(0, ROWS, one, 0, unroll=U_ROW)


def spec_block(b, size=256):
    return pl.ds(pl.multiple_of(b * size, size), size)


def analyse_dense(rows_spec, table, dense):
    def one(b, carry):
        value = get(rows_spec, spec_block(b)).astype(BF16)
        for mode in range(2):
            full = matmul(table[mode], value[128 * mode : 128 * mode + 128]).astype(BF16)
            for part in range(2):
                start = pl.multiple_of(b * 512 + part * 256 + mode * 128, 128)
                dense[pl.ds(start, 128), :] = full[128 * part : 128 * part + 128]
        return carry

    lax.fori_loop(0, LON_BLOCKS, one, 0, unroll=U_BLK)


def store_modes(b, part, modes, parts):
    for lat in range(4):
        tile = modes[32 * lat : 32 * lat + 32]
        px = parts[0].at[piece_start(b, lat, 48, "xyz")]
        py = parts[1].at[piece_start(b, lat, 48, "yzx")]
        pz = parts[2].at[piece_start(b, lat, 32, "zxy")]
        if part == 0:
            px[0:32, :] = tile[:, 0:128]
            py[0:32, :] = tile[:, 128:256]
        else:
            px[32:48, :] = tile[0:16, 0:128]
            py[32:48, :] = tile[0:16, 128:256]
            pz[0:16, :] = tile[16:32, 0:128]
            pz[16:32, :] = tile[16:32, 128:256]


def load_modes(b, full):
    tiles = [[], []]
    for lat in range(4):
        px = full[0][piece_start(b, lat, 48, "xyz"), :]
        py = full[1][piece_start(b, lat, 48, "yzx"), :]
        pz = full[2][piece_start(b, lat, 32, "zxy"), :]
        tiles[0].append(jnp.concatenate([px[0:32], py[0:32]], axis=1))
        tiles[1].append(jnp.concatenate([px[32:48], py[32:48]], axis=1))
        tiles[1].append(jnp.concatenate([pz[0:16], pz[16:32]], axis=1))
    return jnp.concatenate(tiles[0] + tiles[1], axis=0)


def select_modes(dense, slots, parts):
    def one(b, carry):
        hot = one_hot_turned(slots, b)
        for part in range(2):
            modes = matmul(hot, dense[pl.ds(pl.multiple_of(b * 512 + part * 256, 256), 256), :])
            store_modes(b, part, modes.astype(BF16), parts)
        return carry

    lax.fori_loop(0, LON_BLOCKS, one, 0, unroll=U_BLK)


def build_analysis(slots, table, out, low, high):
    def one(b, carry):
        hot = one_hot_turned(slots, b)
        for part in range(2):
            for mode in range(2):
                value = matmul(
                    hot[:, 128 * mode : 128 * mode + 128],
                    table[mode, 128 * part : 128 * part + 128, :],
                )
                start = pl.multiple_of(b * 256 + part * 128, 128)
                out[pl.ds(start, 128), 128 * mode : 128 * mode + 128] = value.astype(BF16)
        return carry

    lax.fori_loop(low, high, one, 0, unroll=U_BLK)


def build_synthesis(slots, table, out, low, high):
    def one(b, carry):
        hot = one_hot(slots, b)
        for part in range(2):
            for mode in range(2):
                value = matmul(
                    table[mode, :, 128 * part : 128 * part + 128],
                    hot[128 * mode : 128 * mode + 128],
                )
                start = pl.multiple_of(b * 256 + mode * 128, 128)
                out[pl.ds(start, 128), 128 * part : 128 * part + 128] = value.astype(BF16)
        return carry

    lax.fori_loop(low, high, one, 0, unroll=U_BLK)


def analyse_latitude(rows_spec, table, parts):
    def one(b, carry):
        value = get(rows_spec, spec_block(b)).astype(BF16)
        modes = matmul(table[spec_block(b), :], value).astype(BF16)
        for part in range(2):
            store_modes(b, part, modes[128 * part : 128 * part + 128], parts)
        return carry

    lax.fori_loop(0, LON_BLOCKS, one, 0, unroll=U_BLK)


def synthesise_latitude(full, table, rows_spec):
    def one(b, carry):
        put(rows_spec, spec_block(b), matmul(table[spec_block(b), :], load_modes(b, full)))
        return carry

    lax.fori_loop(0, LON_BLOCKS, one, 0, unroll=U_BLK)


def gelu_slope(x):
    c, a = math.sqrt(2.0 / math.pi), 0.044715
    square = x * x
    t = jnp.tanh(x * (c + (c * a) * square))
    half = 0.5 + 0.5 * t
    return half + x * (half * (1.0 - t)) * (c + (3.0 * c * a) * square)


def hidden_gradient(out_grad, w2, hidden, low, high):
    def one(i, carry):
        grad = out_grad[pl.ds(i * GROUP, GROUP)].reshape(GROUP * ROWS, CH)
        here = pl.ds(pl.multiple_of(i * (GROUP * ROWS), GROUP * ROWS), GROUP * ROWS)
        for k in range(HID // CHUNK):
            cols = slice(CHUNK * k, CHUNK * k + CHUNK)
            hidden[here, cols] = matmul(grad, w2[cols, :], (1, 1)).astype(BF16)
        return carry

    lax.fori_loop(low, high, one, 0)


def pointwise(points, hidden, w1, low, high):
    def one(i, carry):
        here = pl.ds(pl.multiple_of(i * (GROUP * ROWS), GROUP * ROWS), GROUP * ROWS)
        value = get(points, here).astype(BF16)
        total = None
        for k in range(HID // CHUNK):
            cols = slice(CHUNK * k, CHUNK * k + CHUNK)
            pre = matmul(value, w1[:, cols])
            pre_grad = (gelu_slope(pre) * hidden[here, cols].astype(F32)).astype(BF16)
            term = matmul(pre_grad, w1[:, cols], (1, 1))
            total = term if total is None else total + term
        put(points, here, total)
        return carry

    lax.fori_loop(low, high, one, 0)


def lane_match(spread_high):
    channel = lax.broadcasted_iota(jnp.int32, (CH, CH), 0) & (BS - 1)
    lane = lax.broadcasted_iota(jnp.int32, (CH, CH), 1)
    half = lax.shift_right_logical(lane, 4) if spread_high else lane & (BS - 1)
    return jnp.where(channel == half, 1.0, 0.0).astype(BF16)


def lane_sum(over_low):
    lane = lax.broadcasted_iota(jnp.int32, (CH, CH), 0)
    channel = lax.broadcasted_iota(jnp.int32, (CH, CH), 1) & (BS - 1)
    half = lax.shift_right_logical(lane, 4) if over_low else lane & (BS - 1)
    return jnp.where(channel == half, 1.0, 0.0).astype(BF16)


def block_mask():
    beta = lax.broadcasted_iota(jnp.int32, (CH // BS, CH), 0)
    channel = lax.broadcasted_iota(jnp.int32, (CH // BS, CH), 1)
    return jnp.where(beta == lax.shift_right_logical(channel, 4), 1.0, 0.0)


def exact(value, ones):
    high = value.astype(BF16)
    low = (value - high.astype(F32)).astype(BF16)
    return matmul(high, ones) + matmul(low, ones)


MIX = 8


def spread(modes, match, out):
    mask = block_mask()[None]

    def one(i, carry):
        value = modes[pl.ds(pl.multiple_of(i * MIX, MIX), MIX), :]
        wide = (value[:, None, :] * mask).reshape(MIX * BS, CH)
        out[pl.ds(pl.multiple_of(i * (MIX * BS), MIX * BS), MIX * BS), :] = exact(wide, match)
        return carry

    lax.fori_loop(0, 2 * KEEP // MIX, one, 0, unroll=2)


def spread_rows(i, part):
    return pl.ds(pl.multiple_of(part * (KEEP * BS) + i * (MIX * BS), MIX * BS), MIX * BS)


def mix(wide, weight, conjugate, sums, out):
    mask = block_mask()[None]

    def one(i, carry):
        re, im = wide[spread_rows(i, 0), :], wide[spread_rows(i, 1), :]
        wr, wi = (
            weight[pl.ds(i * MIX, MIX), part].astype(F32).reshape(MIX * BS, CH) for part in range(2)
        )
        if conjugate:
            terms = re * wr + im * wi, im * wr - re * wi
        else:
            terms = re * wr - im * wi, re * wi + im * wr
        for part, term in enumerate(terms):
            total = exact(term, sums).reshape(MIX, BS, CH) * mask
            start = pl.multiple_of(part * KEEP + i * MIX, MIX)
            out[pl.ds(start, MIX), :] = jnp.sum(total, axis=1)
        return carry

    lax.fori_loop(0, KEEP // MIX, one, 0, unroll=2)


def weight_gradient(wide_in, wide_grad, out):
    def one(i, carry):
        ar, ai = wide_in[spread_rows(i, 0), :], wide_in[spread_rows(i, 1), :]
        br, bi = wide_grad[spread_rows(i, 0), :], wide_grad[spread_rows(i, 1), :]
        here = pl.ds(i * MIX, MIX)
        out[here, 0] = (ar * br + ai * bi).reshape(MIX, BS, CH)
        out[here, 1] = (ar * bi - ai * br).reshape(MIX, BS, CH)
        return carry

    lax.fori_loop(0, KEEP // MIX, one, 0)


KEPT_PIECE = ((8, "xyz"),)


def own_slots(at, kept):
    lat = lax.rem(at["z"], 2) * 2 + at["core"]
    value = jnp.concatenate([kept[...]] * 4, axis=1)
    slot = (value & 1) * KLAT + lat * KEEP + lax.shift_right_logical(value, 1)
    lane = lax.broadcasted_iota(jnp.int32, (1, 128), 1)
    return jnp.where(lax.shift_right_logical(lane, 5) == lat, slot.astype(F32), 0.0)


def collect_slots(full, slots):
    for b in range(LON_BLOCKS):
        x, zhi, y = b // 8, b // 4 % 2, b % 4
        first = ((x * 4 + y) * 4 + zhi * 2) * 8
        total = full[first : first + 8, :]
        for start in (first + 8, first + 512, first + 520):
            total = total + full[start : start + 8, :]
        slots[b : b + 1, :] = total[0:1]


def kernel(
    fwd_scale,
    syn_scale,
    field,
    out_grad_hbm,
    weight_hbm,
    w1_hbm,
    w2_hbm,
    kept,
    basis_hbm,
    back_hbm,
    plain_hbm,
    doubled_hbm,
    plain_back_hbm,
    doubled_back_hbm,
    input_grad,
    spectral_grad,
    *scratch,
):
    scratch = list(scratch)

    def take(n):
        taken = scratch[:n]
        del scratch[:n]
        return taken

    out_grad, weight, w1, w2, basis, basis_back, plain, doubled, plain_back, doubled_back = take(10)
    (load_sems,) = take(1)
    points, rows_spec, parts, full = take(2), take(2), take(3), take(3)
    tables, hidden, slots, kept_full, modes, mixed, wide_in, wide_grad = take(8)
    kept_sems, full_sems, scatter = take(4), take(4), scratch
    analysis, synthesis = tables.at[0:8192], tables.at[8192:16384]

    at = own_place()
    lat, lon = lax.axis_index("lat"), lax.axis_index("lon")
    greeted = greet(at)
    loads = []
    for i, (src, dst) in enumerate(
        [
            (basis_hbm.at[lon], basis),
            (doubled_hbm.at[lat], doubled),
            (plain_hbm.at[lat], plain),
            (plain_back_hbm.at[lat], plain_back),
            (weight_hbm, weight),
            (w2_hbm, w2),
            (out_grad_hbm, out_grad),
            (back_hbm.at[lon], basis_back),
            (w1_hbm, w1),
            (doubled_back_hbm.at[lat], doubled_back),
        ]
    ):
        copy = pltpu.make_async_copy(src, dst, load_sems.at[i])
        copy.start()
        loads.append(copy)
    here = rows((at["core"] * 64 + index_of(at, "xyz")) * 8, 8)
    kept_full[here, :] = jnp.broadcast_to(own_slots(at, kept), (8, 128))
    fill_points(field, points)
    pl.semaphore_wait(pltpu.get_barrier_semaphore(), greeted)

    def first_longitude():
        loads[0].wait()
        analyse_longitude(points, basis, rows_spec)

    def first_dense():
        loads[1].wait()
        analyse_dense(rows_spec, doubled, tables)

    run(gather(at, KEPT_PIECE, (kept_full,), kept_sems), first_longitude, first_dense)
    collect_slots(kept_full, slots)
    select_modes(tables, slots, parts)

    def wait_tables():
        for copy in loads[2:]:
            copy.wait()

    def build(table, turned, out, low, high):
        (build_analysis if turned else build_synthesis)(slots, table, out, low, high)

    def work_a():
        wait_tables()
        build(plain, True, analysis, 0, LON_BLOCKS)

    run(
        reduce_scatter(at, parts, fwd_scale, modes, scatter),
        work_a,
        lambda: build(plain_back, False, synthesis, 0, LON_BLOCKS // 2),
        lambda: build(plain_back, False, synthesis, LON_BLOCKS // 2, LON_BLOCKS),
    )
    spread(modes, lane_match(True), wide_in)
    mix(wide_in, weight, False, lane_sum(False), mixed)
    put_own(at, mixed[...].astype(BF16), full)
    groups = LONS // GROUP
    run(
        gather(at, PIECES, full, full_sems),
        lambda: hidden_gradient(out_grad, w2, hidden, 0, groups // 3),
        lambda: hidden_gradient(out_grad, w2, hidden, groups // 3, 2 * groups // 3),
        lambda: hidden_gradient(out_grad, w2, hidden, 2 * groups // 3, groups),
    )
    synthesise_latitude(full, synthesis, rows_spec)
    synthesise_longitude(rows_spec, basis_back, points, syn_scale)
    pointwise(points, hidden, w1, 0, groups)
    analyse_longitude(points, basis, rows_spec)
    analyse_latitude(rows_spec, analysis, parts)
    run(
        reduce_scatter(at, parts, syn_scale, modes, scatter),
        lambda: build(doubled_back, False, synthesis, 0, LON_BLOCKS),
    )
    spread(modes, lane_match(False), wide_grad)
    mix(wide_grad, weight, True, lane_sum(True), mixed)
    put_own(at, mixed[...].astype(BF16), full)
    run(
        gather(at, PIECES, full, full_sems),
        lambda: weight_gradient(wide_in, wide_grad, spectral_grad),
    )
    synthesise_latitude(full, synthesis, rows_spec)
    synthesise_longitude(rows_spec, basis_back, points, fwd_scale)

    def finish(j, carry):
        part = get(points, spec_block(j, ROWS))
        input_grad[j] = (out_grad[j].astype(F32) + part).astype(BF16)
        return carry

    lax.fori_loop(0, LONS, finish, 0, unroll=U_FILL)


def kernel_scratch():
    v, dma = pltpu.VMEM, pltpu.SemaphoreType.DMA
    return [
        v((LONS, ROWS, CH), BF16),
        v((KEEP, 2, CH // BS, BS * BS), BF16),
        v((CH, HID), BF16),
        v((HID, CH), BF16),
        v((2 * KM, LONS_PAD), BF16),
        v((LONS_PAD, 2 * KM), BF16),
        v((2, 2 * KLAT, 2 * ROWS), BF16),
        v((2, 2 * KLAT, 2 * ROWS), BF16),
        v((2, 2 * ROWS, 2 * KLAT), BF16),
        v((2, 2 * ROWS, 2 * KLAT), BF16),
        dma((10,)),
        *[v((LONS_PAD * ROWS, 128), F32)] * 2,
        *[v((LON_BLOCKS * 4 * ROWS, 128), F32)] * 2,
        *[v((128 * size, 128), BF16) for size, _ in PIECES] * 2,
        v((16384, CH), BF16),
        v((LONS * ROWS, HID), BF16),
        v((LON_BLOCKS, 128), F32),
        v((1024, 128), F32),
        v((2 * KEEP, CH), F32),
        v((2 * KEEP, CH), F32),
        v((2 * KEEP * BS, CH), F32),
        v((2 * KEEP * BS, CH), F32),
        *gather_sems(KEPT_PIECE),
        *gather_sems(PIECES),
        *scatter_scratch(),
    ]


def longitude_tables(lon_total):
    j = np.arange(lon_total).reshape(-1, LONS)
    j = np.pad(j, ((0, 0), (0, LONS_PAD - LONS)))
    q = np.arange(2 * KM)
    angles = (j[:, None, :] * (q // 2)[None, :, None] % lon_total) * (2.0 * math.pi / lon_total)
    basis = np.where((q % 2)[None, :, None] == 0, np.cos(angles), -np.sin(angles))
    basis[:, :, LONS:] = 0.0
    basis = basis.astype(np.float32)
    return jnp.asarray(basis, BF16), jnp.asarray(np.swapaxes(basis, 1, 2), BF16)


def latitude_tables(lat_total):
    wave = np.arange(KLAT) - KLAT // 2

    def angles(ids):
        return (wave[None, :, None] * ids[:, None, :] % (2 * lat_total)) * (math.pi / lat_total)

    ids = np.arange(lat_total).reshape(-1, ROWS)
    upper, lower = angles(ids), angles(2 * lat_total - 1 - ids)
    cu, su, cl, sl = np.cos(upper), np.sin(upper), np.cos(lower), np.sin(lower)

    def table(c, s):
        top, bottom = np.concatenate([c, s], axis=2), np.concatenate([-s, c], axis=2)
        return np.concatenate([top, bottom], axis=1)

    plain = np.stack([table(cu, su)] * 2, axis=1)
    doubled = np.stack([table(cu + cl, su + sl), table(cu - cl, su - sl)], axis=1)
    tables = []
    for value in (plain, doubled, np.swapaxes(plain, 2, 3), np.swapaxes(doubled, 2, 3)):
        tables.append(jnp.asarray(value.astype(np.float32), BF16))
    return tables


def body(in_field, out_grad, spec_weight, inner_weight, output_projection_weight, kept_modes):
    lat_parts, lon_parts = lax.axis_size("lat"), lax.axis_size("lon")
    lat_total, lon_total = ROWS * lat_parts, LONS * lon_parts
    fwd_scale = 1.0 / math.sqrt(2 * lat_total * lon_total)
    syn_scale = 1.0 / math.sqrt(KEEP * lat_parts * lon_parts)
    hbm = pl.BlockSpec(memory_space=pl.ANY)
    input_grad, spectral_grad = pl.pallas_call(
        functools.partial(kernel, fwd_scale, syn_scale),
        out_shape=(
            jax.ShapeDtypeStruct((LONS, ROWS, CH), BF16),
            jax.ShapeDtypeStruct((KEEP, 2, CH // BS, BS * BS), F32),
        ),
        in_specs=[VMEM] + [hbm] * 4 + [VMEM] + [hbm] * 6,
        out_specs=(VMEM, VMEM),
        scratch_shapes=kernel_scratch(),
        compiler_params=pltpu.CompilerParams(
            collective_id=0, has_side_effects=True, vmem_limit_bytes=LIMIT
        ),
        name="layer_gradients",
    )(
        jnp.swapaxes(in_field, 0, 1),
        jnp.swapaxes(out_grad, 0, 1),
        spec_weight,
        inner_weight,
        output_projection_weight,
        kept_modes.reshape(1, KEEP),
        *longitude_tables(lon_total),
        *latitude_tables(lat_total),
    )
    return jnp.swapaxes(input_grad, 0, 1), spectral_grad


def solution(mesh):
    return jax.shard_map(
        body,
        mesh=mesh,
        in_specs=(
            P("lat", "lon", None),
            P("lat", "lon", None),
            P(("lat", "lon"), None, None, None),
            P(),
            P(),
            P(("lat", "lon")),
        ),
        out_specs=(P("lat", "lon", None), P(("lat", "lon"), None, None, None)),
        check_vma=False,
    )
```

time: 296 us -> 155 us (0.52)
  Pallas kernels: 262 us -> 149 us
  local copies, waits for them, and re-layouts: 19 us -> 3.72 us
  other arithmetic: 12.5 us -> 0 us
    pallas_call x8 -> x1, Pallas kernels: 262 us -> 149 us  [body(): pl.pallas_call(functools.partial(kernel, fwd_scale, syn_scale), out_shape...]
    unnamed x9 -> x4, local copies, waits for them, and re-layouts: 9.62 us -> 3.72 us
    dot_general x2 -> x0, other arithmetic: 3.31 us -> none  [the longest x1 2.23 us: mix_back(): return jnp.einsum('qbo,qbio->qbi', a, b, precision=highest)]
where the time goes in v2:
time: 155 us; the launch traced here: 154 us
  Pallas kernels  149 us (96%)
  local copies, waits for them, and re-layouts  3.72 us (2%)
    pallas_call x1, Pallas kernels, body(): pl.pallas_call(functools.partial(kernel, fwd_scale, syn_scale), out_shape...  149 us
    unnamed x4, local copies, waits for them, and re-layouts  3.72 us

profile of v2, /device:TPU:0, one launch (start us, length us, event | category | flops | bytes accessed | tf_op | source)
XLA Modules:
  0.0 153.6 jit_solution(9003597018584648165)
XLA Ops:
  0.6 149.3 %layer_gradients.1 = (bf16[45,64,256]{2,1,0:T(8,128)(2,1)}, f32[32,2,16,256]{3,2,1,0:T(8,128)}) custom-call(bf16[45,64,256]{2,1,0:T(8,128)(2,1)} %bitcast.4, bf16[45,64,256]{2,1,0:T(8,128)(2,1)} %bitcast.5, bf16[32,2,16,256]{3,2,1,0:T(8,128)(2,1)} %weight_hbm.1, bf16[256,1024]{1,0:T(8,128)(2,1)} %w1_hbm.1, bf16[1024,256]{1,0:T(8,128)(2,1)} %w2_hbm.1, ...), custom_call_target="tpu_custom_call" | custom-call | tf_op jit(solution)/shard_map/layer_gradients/pallas_call | solution.py:738
  149.9 0.0 copy-start
  149.9 2.7 %copy.16 = bf16[64,45,256]{2,0,1:T(8,128)(2,1)} copy(bf16[64,45,256]{2,0,1:T(8,128)(2,1)} %bitcast.6) | data formatting | bytes 2949120
  152.7 0.0 copy-done
  152.7 1.0 copy.17
Async XLA Ops:
  149.9 2.8 %copy-start = (f32[32,2,16,256]{3,2,1,0:T(8,128)S(1)}, f32[32,2,16,256]{3,2,1,0:T(8,128)}, u32[]{:S(2)}) copy-start(f32[32,2,16,256]{3,2,1,0:T(8,128)} %get-tuple-element.9) | copy-start | bytes 3145732

commit v3 on v2

v3 whole, which is shorter than its diff:
```python
import functools
import math

import jax
import jax.numpy as jnp
import numpy as np
from jax import lax
from jax.experimental import pallas as pl
from jax.experimental.pallas import tpu as pltpu
from jax.sharding import PartitionSpec as P

BS = 16
KM = 64
KLAT = 128
RING = 4
STEPS = (2, 1, 3)
ROWS, LONS, CH, HID = 64, 45, 256, 1024
LONS_PAD = 48
LON_BLOCKS = 32
KEEP = 32
HALVES = (
    ((32, "xyz"), (16, "yzx"), (16, "zxy")),
    ((32, "yzx"), (16, "xyz"), (16, "zxy")),
)
HALF = 128
STRIDE = 72
MESH = pl.DeviceIdType.MESH
F32, BF16 = jnp.float32, jnp.bfloat16
VMEM = pl.BlockSpec(memory_space=pltpu.VMEM)
LIMIT = 60 << 20
U_FILL, U_ROW, U_BLK, U_BUILD, GROUP, CHUNK, WORK = 5, 16, 8, 4, 9, 256, 3


def matmul(a, b, contract=(1, 0)):
    dims = (((contract[0],), (contract[1],)), ((), ()))
    return lax.dot_general(a, b, dims, preferred_element_type=F32)


def own_place():
    lat, lon = lax.axis_index("lat"), lax.axis_index("lon")
    return {
        "x": lax.div(lon, 8),
        "y": lax.rem(lon, 4),
        "z": lax.rem(lax.div(lon, 4), 2) * 2 + lax.div(lat, 2),
        "core": lax.rem(lat, 2),
    }


def moved(at, axis, step):
    return {**at, axis: lax.rem(at[axis] + step, 2 if axis == "core" else RING)}


def device_of(at):
    return (lax.rem(at["z"], 2) * 2 + at["core"], at["x"] * 8 + lax.div(at["z"], 2) * 4 + at["y"])


def greet(at):
    partners = [moved(at, axis, step) for axis in "xyz" for step in STEPS] + [moved(at, "core", 1)]
    partners += [moved(moved(at, "y", dy), "z", dz) for dy in STEPS for dz in STEPS]
    for partner in partners:
        pl.semaphore_signal(
            pltpu.get_barrier_semaphore(),
            inc=1,
            device_id=device_of(partner),
            device_id_type=MESH,
        )
    return len(partners)


def send(src, dst, sems, target):
    copy = pltpu.make_async_remote_copy(
        src_ref=src,
        dst_ref=dst,
        send_sem=sems[0],
        recv_sem=sems[1],
        device_id=device_of(target),
        device_id_type=MESH,
    )
    copy.start()
    return copy


def rows(start, size):
    return pl.ds(pl.multiple_of(start, math.gcd(size, 16)), size)


def index_of(at, order):
    index = 0
    for name in order:
        index = index * RING + at[name]
    return index


def pair_of_sems(*shape):
    return [pltpu.SemaphoreType.DMA(shape)] * 2


def gather(at, pieces, full, sems):
    ring_send, ring_recv, core_send, core_recv = sems
    bases = [at["core"] * (64 * size) for size, _ in pieces]
    sibling = moved(at, "core", 1)
    pending, across = [], []
    sent = [[] for _ in pieces]

    def across_core(i, s, step):
        size, order = pieces[i]
        slab = lax.rem(at[order[0]] + step, RING)
        here = full[i].at[rows(bases[i] + slab * (16 * size), 16 * size)]
        across.append(send(here, here, (core_send.at[i, s], core_recv.at[i, s]), sibling))

    for phase in range(3):
        for i, (size, order) in enumerate(pieces):
            for copy in sent[i]:
                copy.wait_recv()
            block = size * RING**phase
            index = index_of(at, order[: 3 - phase])
            here = full[i].at[rows(bases[i] + index * block, block)]
            sent[i] = [
                send(
                    here,
                    here,
                    (ring_send.at[i, phase, s], ring_recv.at[i, phase, s]),
                    moved(at, order[2 - phase], step),
                )
                for s, step in enumerate(STEPS)
            ]
            pending += sent[i]
        if phase == 2:
            for i in range(len(pieces)):
                across_core(i, 0, 0)
        yield
    for s in (1, 2, 0):
        for i in range(len(pieces)):
            sent[i][s].wait_recv()
            across_core(i, s + 1, RING - STEPS[s])
    yield
    for copy in across:
        copy.wait_recv()
    for copy in pending + across:
        copy.wait_send()


def scatter_scratch(pieces):
    scratch = [*pair_of_sems(3, 3, 3), *pair_of_sems(3, 4)]
    for size, _ in pieces:
        scratch += [
            pltpu.VMEM((64 * size, HALF), BF16),
            pltpu.VMEM((64 * size, HALF), BF16),
            pltpu.VMEM((3, 16 * size, HALF), BF16),
            pltpu.VMEM((16 * size, HALF), BF16),
            pltpu.VMEM((3, 4 * size, HALF), BF16),
            pltpu.VMEM((4 * size, HALF), BF16),
            pltpu.VMEM((3, size, HALF), BF16),
        ]
    return scratch


def reduce_scatter(at, pieces, parts, scale, out, scratch):
    ring_send, ring_recv, core_send, core_recv = scratch[:4]
    bufs = [scratch[4 + 7 * i : 11 + 7 * i] for i in range(3)]
    sibling = moved(at, "core", 1)
    pending, across = [], {}
    for s, step in enumerate(STEPS + (0,)):
        for i, (size, order) in enumerate(pieces):
            slab = lax.rem(at[order[0]] + step, RING) * (16 * size)
            across[s, i] = send(
                parts[i].at[rows((1 - at["core"]) * (64 * size) + slab, 16 * size)],
                bufs[i][0].at[rows(slab, 16 * size)],
                (core_send.at[i, s], core_recv.at[i, s]),
                sibling,
            )
    yield
    sent = [[], [], []]
    for s, step in enumerate(STEPS + (0,)):
        for i, (size, order) in enumerate(pieces):
            slab = lax.rem(at[order[0]] + step, RING) * (16 * size)
            across[s, i].wait_recv()
            here = rows(slab, 16 * size)
            own = parts[i][rows(at["core"] * (64 * size) + slab, 16 * size), :]
            bufs[i][1][here, :] = (own.astype(F32) + bufs[i][0][here, :].astype(F32)).astype(BF16)
            if step:
                sent[i].append(
                    send(
                        bufs[i][1].at[here],
                        bufs[i][2].at[s],
                        (ring_send.at[i, 0, s], ring_recv.at[i, 0, s]),
                        moved(at, order[0], step),
                    )
                )
    yield
    first = 0
    for phase in range(3):
        first = 0
        for i, (size, order) in enumerate(pieces):
            block = size * RING ** (2 - phase)
            mine, landed = bufs[i][1 + 2 * phase], bufs[i][2 + 2 * phase]
            total = mine[rows(at[order[phase]] * block, block), :].astype(F32)
            for s in (1, 2, 0):
                sent[i][s].wait_recv()
                total = total + landed[s].astype(F32)
            pending += sent[i]
            if phase == 2:
                out[first : first + size, :] = total * scale
                first += size
                continue
            after = bufs[i][3 + 2 * phase]
            after[...] = total.astype(BF16)
            small = block // RING
            axis = order[phase + 1]
            sent[i] = [
                send(
                    after.at[rows(lax.rem(at[axis] + step, RING) * small, small)],
                    bufs[i][4 + 2 * phase].at[s],
                    (ring_send.at[i, phase + 1, s], ring_recv.at[i, phase + 1, s]),
                    moved(at, axis, step),
                )
                for s, step in enumerate(STEPS)
            ]
        if phase < 2:
            yield
    for copy in pending + list(across.values()):
        copy.wait_send()


def put_own(at, pieces, modes, full):
    first = 0
    for i, (size, order) in enumerate(pieces):
        here = rows((at["core"] * 64 + index_of(at, order)) * size, size)
        full[i][here, :] = modes[first : first + size]
        first += size


def own_slots(at, kept):
    lat = lax.rem(at["z"], 2) * 2 + at["core"]
    value = jnp.concatenate([kept[...]] * 4, axis=1)
    slot = (value & 1) * KLAT + lat * KEEP + lax.shift_right_logical(value, 1)
    lane = lax.broadcasted_iota(jnp.int32, (1, 128), 1)
    own = jnp.where(lax.shift_right_logical(lane, 5) == lat, slot.astype(F32), 0.0)
    return jnp.broadcast_to(own, (8, 128))


def gather_slots(at, own, other, full, sems):
    core_send, core_recv, line_send, line_recv, plane_send, plane_recv = sems
    copies = [send(own, other, (core_send.at[0], core_recv.at[0]), moved(at, "core", 1))]
    copies[0].wait_recv()
    mine = rows(index_of(at, "yzx") * 8, 8)
    full[mine, :] = own[...] + other[...]
    line = [
        send(full.at[mine], full.at[mine], (line_send.at[s], line_recv.at[s]), moved(at, "x", step))
        for s, step in enumerate(STEPS)
    ]
    yield
    for copy in line:
        copy.wait_recv()
    here = full.at[rows(index_of(at, "yz") * 32, 32)]
    plane = []
    for dy, dz in ((2, 2), (2, 1), (2, 3), (1, 2), (3, 2), (1, 1), (1, 3), (3, 1), (3, 3)):
        plane.append((dy, dz))
    for step in STEPS:
        plane += [(step, 0), (0, step)]
    plane = [
        send(
            here,
            here,
            (plane_send.at[dy, dz], plane_recv.at[dy, dz]),
            moved(moved(at, "y", dy), "z", dz),
        )
        for dy, dz in plane
    ]
    yield
    for copy in plane:
        copy.wait_recv()
    for copy in copies + line + plane:
        copy.wait_send()


def collect_slots(full, slots):
    for b in range(LON_BLOCKS):
        x, zhi, y = b // 8, b // 4 % 2, b % 4
        first = ((y * 4 + zhi * 2) * 4 + x) * 8
        total = full[first : first + 8, :] + full[first + 32 : first + 40, :]
        slots[b : b + 1, :] = total[0:1]


def piece_start(b, lat, size, order):
    place = {"x": lax.div(b, 8), "z": lax.rem(lax.div(b, 4), 2) * 2 + lat // 2, "y": lax.rem(b, 4)}
    return rows((lat % 2 * 64 + index_of(place, order)) * size, size)


def group(i):
    return pl.ds(pl.multiple_of(i * STRIDE, 8), ROWS)


def one_hot(slots, b):
    ids = lax.broadcasted_iota(jnp.int32, (256, 128), 0).astype(F32)
    return jnp.where(ids == slots[pl.ds(b, 1), :], 1.0, 0.0).astype(BF16)


def one_hot_turned(slots, b):
    columns = jnp.transpose(jnp.broadcast_to(slots[pl.ds(b, 1), :], (128, 128)))
    ids = lax.broadcasted_iota(jnp.int32, (128, 128), 1).astype(F32)
    hot = [jnp.where(ids == columns - 128.0 * mode, 1.0, 0.0).astype(BF16) for mode in range(2)]
    return jnp.concatenate(hot, axis=1)


def both(halves, where):
    return jnp.concatenate([half[where, :] for half in halves], axis=1)


def fill_points(field, points):
    def one(j, carry):
        value = field[j].astype(F32)
        for h in range(2):
            points[h][group(j), :] = value[:, HALF * h : HALF * h + HALF]
        return carry

    lax.fori_loop(0, LONS, one, 0, unroll=U_FILL)
    for j in range(LONS, LONS_PAD):
        for h in range(2):
            points[h][group(j), :] = jnp.zeros((ROWS, HALF), F32)


def analyse_longitude(points, basis, rows_spec):
    def one(g, carry):
        value = both(points, pl.ds(g, LONS_PAD, stride=STRIDE)).astype(BF16)
        spec = matmul(basis[...], value)
        for h, half in enumerate(rows_spec):
            half[pl.ds(g, 2 * KM, stride=STRIDE), :] = spec[:, HALF * h : HALF * h + HALF]
        return carry

    lax.fori_loop(0, ROWS, one, 0, unroll=U_ROW)


def synthesise_longitude(rows_spec, basis_back, points, scale):
    def one(g, carry):
        spec = rows_spec[pl.ds(g, 2 * KM, stride=STRIDE), :].astype(BF16)
        points[pl.ds(g, LONS_PAD, stride=STRIDE), :] = matmul(basis_back[...], spec) * scale
        return carry

    lax.fori_loop(0, ROWS, one, 0, unroll=U_ROW)


def spec_block(b, size=256):
    return pl.ds(pl.multiple_of(b * size, size), size)


def analyse_dense(rows_spec, table, dense):
    def one(b, carry):
        for mode in range(2):
            value = jnp.concatenate(
                [both(rows_spec, group(b * 4 + mode * 2 + part)) for part in range(2)], axis=0
            )
            full = matmul(table[mode], value.astype(BF16)).astype(BF16)
            for part in range(2):
                start = pl.multiple_of(b * 512 + part * 256 + mode * 128, 128)
                dense[pl.ds(start, 128), :] = full[128 * part : 128 * part + 128]
        return carry

    lax.fori_loop(0, LON_BLOCKS, one, 0, unroll=U_BLK)


def store_modes(b, part, modes, pieces, parts):
    for lat in range(4):
        tile = modes[32 * lat : 32 * lat + 32]
        starts = [piece_start(b, lat, *piece) for piece in pieces]
        if part == 0:
            parts[0][starts[0], :] = tile
        else:
            parts[1][starts[1], :] = tile[0:16]
            parts[2][starts[2], :] = tile[16:32]


def load_modes(b, pieces, full):
    tiles = [[], []]
    for lat in range(4):
        values = [full[i][piece_start(b, lat, *piece), :] for i, piece in enumerate(pieces)]
        tiles[0].append(values[0])
        tiles[1] += values[1:]
    return jnp.concatenate(tiles[0] + tiles[1], axis=0)


def select_modes(dense, slots, parts):
    def one(b, carry):
        hot = one_hot_turned(slots, b)
        for part in range(2):
            modes = matmul(hot, dense[spec_block(b * 2 + part), :]).astype(BF16)
            for h in range(2):
                here = modes[:, HALF * h : HALF * h + HALF]
                store_modes(b, part, here, HALVES[h], parts[h])
        return carry

    lax.fori_loop(0, LON_BLOCKS, one, 0, unroll=U_BLK)


def build_analysis(slots, table, out, low, high):
    def one(b, carry):
        hot = one_hot_turned(slots, b)
        for part in range(2):
            for mode in range(2):
                value = matmul(
                    hot[:, 128 * mode : 128 * mode + 128],
                    table[mode, 128 * part : 128 * part + 128, :],
                )
                start = pl.multiple_of(b * 256 + part * 128, 128)
                out[pl.ds(start, 128), 128 * mode : 128 * mode + 128] = value.astype(BF16)
        return carry

    lax.fori_loop(low, high, one, 0, unroll=U_BUILD)


def build_synthesis(slots, table, out, low, high):
    def one(b, carry):
        hot = one_hot(slots, b)
        for part in range(2):
            for mode in range(2):
                value = matmul(
                    table[mode, :, 128 * part : 128 * part + 128],
                    hot[128 * mode : 128 * mode + 128],
                )
                start = pl.multiple_of(b * 256 + mode * 128, 128)
                out[pl.ds(start, 128), 128 * part : 128 * part + 128] = value.astype(BF16)
        return carry

    lax.fori_loop(low, high, one, 0, unroll=U_BUILD)


def analyse_latitude(rows_spec, table, pieces, parts):
    def one(b, carry):
        value = jnp.concatenate([rows_spec[group(b * 4 + q), :] for q in range(4)], axis=0)
        modes = matmul(table[spec_block(b), :], value.astype(BF16)).astype(BF16)
        for part in range(2):
            store_modes(b, part, modes[128 * part : 128 * part + 128], pieces, parts)
        return carry

    lax.fori_loop(0, LON_BLOCKS, one, 0, unroll=U_BLK)


def synthesise_latitude(pieces, full, table, rows_spec):
    def one(b, carry):
        value = matmul(table[spec_block(b), :], load_modes(b, pieces, full))
        for q in range(4):
            rows_spec[group(b * 4 + q), :] = value[ROWS * q : ROWS * q + ROWS]
        return carry

    lax.fori_loop(0, LON_BLOCKS, one, 0, unroll=U_BLK)


def gelu_slope(x):
    c, a = math.sqrt(2.0 / math.pi), 0.044715
    square = x * x
    t = jnp.tanh(x * (c + (c * a) * square))
    half = 0.5 + 0.5 * t
    return half + x * (half * (1.0 - t)) * (c + (3.0 * c * a) * square)


def hidden_gradient(out_grad, w2, hidden, low, high):
    def one(i, carry):
        grad = out_grad[pl.ds(i * GROUP, GROUP)].reshape(GROUP * ROWS, CH)
        here = pl.ds(pl.multiple_of(i * (GROUP * ROWS), GROUP * ROWS), GROUP * ROWS)
        for k in range(HID // CHUNK):
            cols = slice(CHUNK * k, CHUNK * k + CHUNK)
            hidden[here, cols] = matmul(grad, w2[cols, :], (1, 1)).astype(BF16)
        return carry

    lax.fori_loop(low, high, one, 0)


def pointwise(points, hidden, w1, low, high):
    def one(i, carry):
        here = pl.ds(pl.multiple_of(i * (GROUP * ROWS), GROUP * ROWS), GROUP * ROWS)
        value = [both(points, group(i * GROUP + j)).astype(BF16) for j in range(GROUP)]
        value = jnp.concatenate(value, axis=0)
        total = None
        for k in range(HID // CHUNK):
            cols = slice(CHUNK * k, CHUNK * k + CHUNK)
            pre = matmul(value, w1[:, cols])
            pre_grad = (gelu_slope(pre) * hidden[here, cols].astype(F32)).astype(BF16)
            term = matmul(pre_grad, w1[:, cols], (1, 1))
            total = term if total is None else total + term
        for j in range(GROUP):
            for h in range(2):
                points[h][group(i * GROUP + j), :] = total[
                    ROWS * j : ROWS * j + ROWS, HALF * h : HALF * h + HALF
                ]
        return carry

    lax.fori_loop(low, high, one, 0)


BETAS = HALF // BS
MIX = 16


def match_lanes(high, lane_first):
    shape = (CH, HALF) if lane_first else (HALF, CH)
    lane = lax.broadcasted_iota(jnp.int32, shape, 0 if lane_first else 1)
    channel = lax.broadcasted_iota(jnp.int32, shape, 1 if lane_first else 0) & (BS - 1)
    half = lax.shift_right_logical(lane, 4) if high else lane & (BS - 1)
    return jnp.where(channel == half, 1.0, 0.0).astype(BF16)


def block_mask():
    beta = lax.broadcasted_iota(jnp.int32, (BETAS, HALF), 0)
    channel = lax.broadcasted_iota(jnp.int32, (BETAS, HALF), 1)
    return jnp.where(beta == lax.shift_right_logical(channel, 4), 1.0, 0.0)[None]


def exact(value, ones):
    high = value.astype(BF16)
    low = (value - high.astype(F32)).astype(BF16)
    return matmul(high, ones) + matmul(low, ones)


def widen_weight(weight, wide):
    def one(e, carry):
        for part in range(2):
            value = weight[e, part].astype(F32)
            for h in range(2):
                start = pl.multiple_of((part * KEEP + e) * BETAS, BETAS)
                wide[h][pl.ds(start, BETAS), :] = value[BETAS * h : BETAS * h + BETAS]
        return carry

    lax.fori_loop(0, KEEP, one, 0, unroll=4)


def spread(modes, high, out):
    mask, match = block_mask(), match_lanes(high, False)
    for i in range(2 * KEEP // MIX):
        value = modes[MIX * i : MIX * i + MIX, :]
        wide = (value[:, None, :] * mask).reshape(MIX * BETAS, HALF)
        out[MIX * BETAS * i : MIX * BETAS * (i + 1), :] = exact(wide, match)


def mixing_rows(i):
    return [
        slice((part * KEEP + MIX * i) * BETAS, (part * KEEP + MIX * (i + 1)) * BETAS)
        for part in range(2)
    ]


def mix(wide, weight, backward):
    mask, sums = block_mask(), match_lanes(backward, True)
    out = [[], []]
    for i in range(KEEP // MIX):
        first, second = mixing_rows(i)
        re, im, wr, wi = wide[first, :], wide[second, :], weight[first, :], weight[second, :]
        if backward:
            terms = re * wr + im * wi, im * wr - re * wi
        else:
            terms = re * wr - im * wi, re * wi + im * wr
        for part, term in enumerate(terms):
            total = exact(term, sums).reshape(MIX, BETAS, HALF) * mask
            out[part].append(jnp.sum(total, axis=1))
    return jnp.concatenate(out[0] + out[1], axis=0).astype(BF16)


def weight_gradient(h, wide_in, wide_grad, out):
    for i in range(KEEP // MIX):
        first, second = mixing_rows(i)
        ar, ai, br, bi = wide_in[first, :], wide_in[second, :], wide_grad[first, :], wide_grad[second, :]
        here, betas = slice(MIX * i, MIX * i + MIX), slice(BETAS * h, BETAS * h + BETAS)
        out[here, 0, betas, :] = (ar * br + ai * bi).reshape(MIX, BETAS, CH)
        out[here, 1, betas, :] = (ar * bi - ai * br).reshape(MIX, BETAS, CH)


def kernel(fwd_scale, syn_scale, *refs):
    refs = list(refs)

    def take(n):
        taken = refs[:n]
        del refs[:n]
        return taken

    field_hbm, out_grad_hbm, weight_hbm, w1_hbm, w2_hbm, kept = take(6)
    basis_hbm, back_hbm, plain_hbm, doubled_hbm, plain_back_hbm, doubled_back_hbm = take(6)
    spectral_part, spectral_grad = take(2)
    field, out_grad, weight, w1, w2 = take(5)
    basis, basis_back, plain, doubled, plain_back, doubled_back = take(6)
    (load_sems,) = take(1)
    points, rows_spec = take(2), take(2)
    parts, full = [take(3), take(3)], [take(3), take(3)]
    tables, hidden, slots, own, other, slots_full = take(6)
    modes, weights, wide_in, wide_grad = take(2), take(2), take(2), take(2)
    slot_sems = take(6)
    gather_sems = [take(4), take(4)]
    scatter = [take(25), take(25)]
    analysis, synthesis = tables.at[0:8192], tables.at[8192:16384]

    at = own_place()
    lat, lon = lax.axis_index("lat"), lax.axis_index("lon")
    greeted = greet(at)
    loads = []
    for i, (src, dst) in enumerate(
        [
            (field_hbm, field),
            (basis_hbm.at[lon], basis),
            (doubled_hbm.at[lat], doubled),
            (plain_hbm.at[lat], plain),
            (plain_back_hbm.at[lat], plain_back),
            (weight_hbm, weight),
            (w2_hbm, w2),
            (out_grad_hbm, out_grad),
            (back_hbm.at[lon], basis_back),
            (w1_hbm, w1),
            (doubled_back_hbm.at[lat], doubled_back),
        ]
    ):
        copy = pltpu.make_async_copy(src, dst, load_sems.at[i])
        copy.start()
        loads.append(copy)
    own[...] = own_slots(at, kept)
    loads[0].wait()
    fill_points(field, points)
    pl.semaphore_wait(pltpu.get_barrier_semaphore(), greeted)

    collecting = gather_slots(at, own, other, slots_full, slot_sems)
    next(collecting)
    loads[1].wait()
    analyse_longitude(points, basis, rows_spec)
    next(collecting)
    loads[2].wait()
    analyse_dense(rows_spec, doubled, tables)
    next(collecting, None)
    collect_slots(slots_full, slots)
    select_modes(tables, slots, parts)

    def exchange(h, scale, backward, synthesised):
        wide = (wide_grad if backward else wide_in)[h]
        yield from reduce_scatter(at, HALVES[h], parts[h], scale, modes[h], scatter[h])
        spread(modes[h], not backward, wide)
        put_own(at, HALVES[h], mix(wide, weights[h], backward), full[h])
        yield from gather(at, HALVES[h], full[h], gather_sems[h])
        synthesise_latitude(HALVES[h], full[h], synthesis, rows_spec[h])
        synthesise_longitude(rows_spec[h], basis_back, points[h], synthesised)

    def drive(first, second, work, before=lambda: None):
        next(first)
        before()
        next(second)
        for _ in range(6):
            for task in work[:WORK]:
                task()
            del work[:WORK]
            next(first)
            next(second)
        for task in work:
            task()
        next(first)
        next(first, None)
        next(second)
        next(second, None)

    quarter = LON_BLOCKS // 4
    work = [lambda: [copy.wait() for copy in loads[3:]]]
    for low in range(0, LON_BLOCKS, quarter):
        span = (low, low + quarter)
        work += [
            functools.partial(build_analysis, slots, plain, analysis, *span),
            functools.partial(build_synthesis, slots, plain_back, synthesis, *span),
        ]
    work.insert(1, functools.partial(widen_weight, weight, weights))
    for i in range(LONS // GROUP):
        work.append(functools.partial(hidden_gradient, out_grad, w2, hidden, i, i + 1))
    drive(*[exchange(h, fwd_scale, False, syn_scale) for h in range(2)], work)

    pointwise(points, hidden, w1, 0, LONS // GROUP)

    def analyse(h):
        analyse_longitude(points[h : h + 1], basis, rows_spec[h : h + 1])
        analyse_latitude(rows_spec[h], analysis, HALVES[h], parts[h])

    analyse(0)
    work = []
    for low in range(0, LON_BLOCKS, quarter):
        work.append(
            functools.partial(
                build_synthesis, slots, doubled_back, synthesis, low, low + quarter
            )
        )
        work += [lambda: None] * (WORK - 1)
    for h in range(2):
        work.append(
            functools.partial(weight_gradient, h, wide_in[h], wide_grad[h], spectral_grad)
        )
    drive(
        *[exchange(h, syn_scale, True, fwd_scale) for h in range(2)],
        work,
        lambda: analyse(1),
    )

    def finish(j, carry):
        spectral_part[j] = both(points, group(j)).astype(BF16)
        return carry

    lax.fori_loop(0, LONS, finish, 0, unroll=U_FILL)


def kernel_scratch():
    v = pltpu.VMEM
    pieces = [v((128 * size, HALF), BF16) for half in HALVES for size, _ in half]
    return [
        v((LONS, ROWS, CH), BF16),
        v((LONS, ROWS, CH), BF16),
        v((KEEP, 2, CH // BS, BS * BS), BF16),
        v((CH, HID), BF16),
        v((HID, CH), BF16),
        v((2 * KM, LONS_PAD), BF16),
        v((LONS_PAD, 2 * KM), BF16),
        v((2, 2 * KLAT, 2 * ROWS), BF16),
        v((2, 2 * KLAT, 2 * ROWS), BF16),
        v((2, 2 * ROWS, 2 * KLAT), BF16),
        v((2, 2 * ROWS, 2 * KLAT), BF16),
        pltpu.SemaphoreType.DMA((11,)),
        *[v((LONS_PAD * STRIDE, HALF), F32)] * 2,
        *[v((2 * KM * STRIDE, HALF), F32)] * 2,
        *pieces,
        *pieces,
        v((16384, CH), BF16),
        v((LONS * ROWS, HID), BF16),
        v((LON_BLOCKS, 128), F32),
        v((8, 128), F32),
        v((8, 128), F32),
        v((512, 128), F32),
        *[v((2 * KEEP, HALF), F32)] * 2,
        *[v((2 * KEEP * BETAS, CH), F32)] * 6,
        *pair_of_sems(1),
        *pair_of_sems(3),
        *pair_of_sems(4, 4),
        *[*pair_of_sems(3, 3, 3), *pair_of_sems(3, 4)] * 2,
        *scatter_scratch(HALVES[0]),
        *scatter_scratch(HALVES[1]),
    ]


def longitude_tables(lon_total):
    j = np.arange(lon_total).reshape(-1, LONS)
    j = np.pad(j, ((0, 0), (0, LONS_PAD - LONS)))
    q = np.arange(2 * KM)
    angles = (j[:, None, :] * (q // 2)[None, :, None] % lon_total) * (2.0 * math.pi / lon_total)
    basis = np.where((q % 2)[None, :, None] == 0, np.cos(angles), -np.sin(angles))
    basis[:, :, LONS:] = 0.0
    basis = basis.astype(np.float32)
    return jnp.asarray(basis, BF16), jnp.asarray(np.swapaxes(basis, 1, 2), BF16)


def latitude_tables(lat_total):
    wave = np.arange(KLAT) - KLAT // 2

    def angles(ids):
        return (wave[None, :, None] * ids[:, None, :] % (2 * lat_total)) * (math.pi / lat_total)

    ids = np.arange(lat_total).reshape(-1, ROWS)
    upper, lower = angles(ids), angles(2 * lat_total - 1 - ids)
    cu, su, cl, sl = np.cos(upper), np.sin(upper), np.cos(lower), np.sin(lower)

    def table(c, s):
        top, bottom = np.concatenate([c, s], axis=2), np.concatenate([-s, c], axis=2)
        return np.concatenate([top, bottom], axis=1)

    plain = np.stack([table(cu, su)] * 2, axis=1)
    doubled = np.stack([table(cu + cl, su + sl), table(cu - cl, su - sl)], axis=1)
    tables = []
    for value in (plain, doubled, np.swapaxes(plain, 2, 3), np.swapaxes(doubled, 2, 3)):
        tables.append(jnp.asarray(value.astype(np.float32), BF16))
    return tables


def body(in_field, out_grad, spec_weight, inner_weight, output_projection_weight, kept_modes):
    lat_parts, lon_parts = lax.axis_size("lat"), lax.axis_size("lon")
    lat_total, lon_total = ROWS * lat_parts, LONS * lon_parts
    fwd_scale = 1.0 / math.sqrt(2 * lat_total * lon_total)
    syn_scale = 1.0 / math.sqrt(KEEP * lat_parts * lon_parts)
    hbm = pl.BlockSpec(memory_space=pl.ANY)
    spectral_part, spectral_grad = pl.pallas_call(
        functools.partial(kernel, fwd_scale, syn_scale),
        out_shape=(
            jax.ShapeDtypeStruct((LONS, ROWS, CH), BF16),
            jax.ShapeDtypeStruct((KEEP, 2, CH // BS, BS * BS), F32),
        ),
        in_specs=[hbm] * 5 + [VMEM] + [hbm] * 6,
        out_specs=(VMEM, VMEM),
        scratch_shapes=kernel_scratch(),
        compiler_params=pltpu.CompilerParams(
            collective_id=0, has_side_effects=True, vmem_limit_bytes=LIMIT
        ),
        name="layer_gradients",
    )(
        jnp.swapaxes(in_field, 0, 1),
        jnp.swapaxes(out_grad, 0, 1),
        spec_weight,
        inner_weight,
        output_projection_weight,
        kept_modes.reshape(1, KEEP),
        *longitude_tables(lon_total),
        *latitude_tables(lat_total),
    )
    part = jnp.swapaxes(spectral_part, 0, 1)
    input_grad = (out_grad.astype(F32) + part.astype(F32)).astype(BF16)
    return input_grad, spectral_grad


def solution(mesh):
    return jax.shard_map(
        body,
        mesh=mesh,
        in_specs=(
            P("lat", "lon", None),
            P("lat", "lon", None),
            P(("lat", "lon"), None, None, None),
            P(),
            P(),
            P(("lat", "lon")),
        ),
        out_specs=(P("lat", "lon", None), P(("lat", "lon"), None, None, None)),
        check_vma=False,
    )
```

time: 155 us -> 131 us (0.85)
  Pallas kernels: 149 us -> 125 us
  other arithmetic: 0 us -> 3.2 us
  local copies, waits for them, and re-layouts: 3.72 us -> 0.98 us
    pallas_call x1, Pallas kernels: 149 us -> 125 us  [body(): pl.pallas_call(functools.partial(kernel, fwd_scale, syn_scale), out_shape...]
    convert_element_type x0 -> x1, other arithmetic: none -> 3.2 us  [body(): input_grad = (out_grad.astype(F32) + part.astype(F32)).astype(BF16)]
    unnamed x4 -> x5, local copies, waits for them, and re-layouts: 3.72 us -> 0.98 us
where the time goes in v3:
time: 131 us; the launch traced here: 130 us
  Pallas kernels  125 us (95%)
  other arithmetic  3.2 us (2%)
    pallas_call x1, Pallas kernels, body(): pl.pallas_call(functools.partial(kernel, fwd_scale, syn_scale), out_shape...  125 us
    convert_element_type x1, other arithmetic, body(): input_grad = (out_grad.astype(F32) + part.astype(F32)).astype(BF16)  3.2 us

profile of v3, /device:TPU:0, one launch (start us, length us, event | category | flops | bytes accessed | tf_op | source)
XLA Modules:
  0.0 130.2 jit_solution(1624565996259327398)
XLA Ops:
  0.6 0.0 copy-start
  0.6 125.4 %layer_gradients.1 = (bf16[45,64,256]{2,1,0:T(8,128)(2,1)}, f32[32,2,16,256]{3,2,1,0:T(8,128)}) custom-call(bf16[45,64,256]{2,1,0:T(8,128)(2,1)} %bitcast.8, bf16[45,64,256]{2,1,0:T(8,128)(2,1)} %bitcast.7, bf16[32,2,16,256]{3,2,1,0:T(8,128)(2,1)} %refs_2_.1, bf16[256,1024]{1,0:T(8,128)(2,1)} %refs_3_.1, bf16[1024,256]{1,0:T(8,128)(2,1)} %refs_4_.1, ...), custom_call_target="tpu_custom_call" | custom-call | tf_op jit(solution)/shard_map/layer_gradients/pallas_call | solution.py:774
  126.0 0.0 copy-done
  126.0 0.0 copy-start.1
  126.0 3.2 %fusion = bf16[64,45,256]{2,0,1:T(8,128)(2,1)} fusion(bf16[45,64,256]{2,1,0:T(8,128)(2,1)} %get-tuple-element.4, bf16[64,45,256]{2,0,1:T(8,128)(2,1)S(1)} %copy-done), kind=kLoop, calls=%fused_computation.1 | loop fusion | flops 2949120 | bytes 4423680 | tf_op jit(solution)/shard_map/convert_element_type | solution.py:798
  129.2 0.0 copy-done.1
  129.2 1.0 copy.15
Async XLA Ops:
  0.6 125.4 %copy-start = (bf16[64,45,256]{2,0,1:T(8,128)(2,1)S(1)}, bf16[64,45,256]{2,0,1:T(8,128)(2,1)}, u32[]{:S(2)}) copy-start(bf16[64,45,256]{2,0,1:T(8,128)(2,1)} %param.13) | copy-start | bytes 4423684
  126.0 3.2 %copy-start.1 = (f32[32,2,16,256]{3,2,1,0:T(8,128)S(1)}, f32[32,2,16,256]{3,2,1,0:T(8,128)}, u32[]{:S(2)}) copy-start(f32[32,2,16,256]{3,2,1,0:T(8,128)} %get-tuple-element.9) | copy-start | bytes 3145732

commit v4 on v3

--- a/solution.py
+++ b/solution.py
@@ -56,7 +56,6 @@
 
 def greet(at):
     partners = [moved(at, axis, step) for axis in "xyz" for step in STEPS] + [moved(at, "core", 1)]
-    partners += [moved(moved(at, "y", dy), "z", dz) for dy in STEPS for dz in STEPS]
     for partner in partners:
         pl.semaphore_signal(
             pltpu.get_barrier_semaphore(),
@@ -240,8 +239,12 @@
 
 
 def gather_slots(at, own, other, full, sems):
-    core_send, core_recv, line_send, line_recv, plane_send, plane_recv = sems
+    core_send, core_recv, line_send, line_recv, plane_send, plane_recv, past = sems
     copies = [send(own, other, (core_send.at[0], core_recv.at[0]), moved(at, "core", 1))]
+    for step in STEPS:
+        pl.semaphore_signal(
+            past, inc=1, device_id=device_of(moved(at, "y", step)), device_id_type=MESH
+        )
     copies[0].wait_recv()
     mine = rows(index_of(at, "yzx") * 8, 8)
     full[mine, :] = own[...] + other[...]
@@ -252,6 +255,7 @@
     yield
     for copy in line:
         copy.wait_recv()
+    pl.semaphore_wait(past, len(STEPS))
     here = full.at[rows(index_of(at, "yz") * 32, 32)]
     plane = []
     for dy, dz in ((2, 2), (2, 1), (2, 3), (1, 2), (3, 2), (1, 1), (1, 3), (3, 1), (3, 3)):
@@ -573,15 +577,16 @@
 
     field_hbm, out_grad_hbm, weight_hbm, w1_hbm, w2_hbm, kept = take(6)
     basis_hbm, back_hbm, plain_hbm, doubled_hbm, plain_back_hbm, doubled_back_hbm = take(6)
-    spectral_part, spectral_grad = take(2)
+    part_hbm, grad_hbm = take(2)
     field, out_grad, weight, w1, w2 = take(5)
     basis, basis_back, plain, doubled, plain_back, doubled_back = take(6)
-    (load_sems,) = take(1)
+    load_sems, store_sems = take(2)
+    (spectral_grad,) = take(1)
     points, rows_spec = take(2), take(2)
     parts, full = [take(3), take(3)], [take(3), take(3)]
     tables, hidden, slots, own, other, slots_full = take(6)
     modes, weights, wide_in, wide_grad = take(2), take(2), take(2), take(2)
-    slot_sems = take(6)
+    slot_sems = take(7)
     gather_sems = [take(4), take(4)]
     scatter = [take(25), take(25)]
     analysis, synthesis = tables.at[0:8192], tables.at[8192:16384]
@@ -624,6 +629,22 @@
     collect_slots(slots_full, slots)
     select_modes(tables, slots, parts)
 
+    stores = []
+
+    def store(src, dst):
+        stores.append(pltpu.make_async_copy(src, dst, store_sems.at[len(stores)]))
+        stores[-1].start()
+
+    def finish(h):
+        lanes = slice(HALF * h, HALF * h + HALF)
+
+        def one(j, carry):
+            field[j, :, lanes] = points[h][group(j), :].astype(BF16)
+            return carry
+
+        lax.fori_loop(0, LONS, one, 0, unroll=U_FILL)
+        store(field.at[:, :, lanes], part_hbm.at[:, :, lanes])
+
     def exchange(h, scale, backward, synthesised):
         wide = (wide_grad if backward else wide_in)[h]
         yield from reduce_scatter(at, HALVES[h], parts[h], scale, modes[h], scatter[h])
@@ -632,6 +653,8 @@
         yield from gather(at, HALVES[h], full[h], gather_sems[h])
         synthesise_latitude(HALVES[h], full[h], synthesis, rows_spec[h])
         synthesise_longitude(rows_spec[h], basis_back, points[h], synthesised)
+        if backward:
+            finish(h)
 
     def drive(first, second, work, before=lambda: None):
         next(first)
@@ -682,17 +705,15 @@
         work.append(
             functools.partial(weight_gradient, h, wide_in[h], wide_grad[h], spectral_grad)
         )
+    work.append(lambda: store(spectral_grad, grad_hbm))
     drive(
         *[exchange(h, syn_scale, True, fwd_scale) for h in range(2)],
         work,
         lambda: analyse(1),
     )
 
-    def finish(j, carry):
-        spectral_part[j] = both(points, group(j)).astype(BF16)
-        return carry
-
-    lax.fori_loop(0, LONS, finish, 0, unroll=U_FILL)
+    for copy in stores:
+        copy.wait()
 
 
 def kernel_scratch():
@@ -711,6 +732,8 @@
         v((2, 2 * ROWS, 2 * KLAT), BF16),
         v((2, 2 * ROWS, 2 * KLAT), BF16),
         pltpu.SemaphoreType.DMA((11,)),
+        pltpu.SemaphoreType.DMA((3,)),
+        v((KEEP, 2, CH // BS, BS * BS), F32),
         *[v((LONS_PAD * STRIDE, HALF), F32)] * 2,
         *[v((2 * KM * STRIDE, HALF), F32)] * 2,
         *pieces,
@@ -726,10 +749,34 @@
         *pair_of_sems(1),
         *pair_of_sems(3),
         *pair_of_sems(4, 4),
+        pltpu.SemaphoreType.REGULAR,
         *[*pair_of_sems(3, 3, 3), *pair_of_sems(3, 4)] * 2,
         *scatter_scratch(HALVES[0]),
         *scatter_scratch(HALVES[1]),
     ]
+
+
+def result_kernel(out_grad, part, grad, out, grad_out):
+    out[...] = (out_grad[...].astype(F32) + part[...].astype(F32)).astype(BF16)
+    grad_out[...] = grad[...]
+
+
+def result_call(out_grad, part, grad):
+    blocks = 4
+    point = pl.BlockSpec((LONS * ROWS // blocks, CH), lambda i: (i, 0))
+    mode = pl.BlockSpec((2 * KEEP * CH // BS // blocks, BS * BS), lambda i: (i, 0))
+    return pl.pallas_call(
+        result_kernel,
+        grid=(blocks,),
+        out_shape=(
+            jax.ShapeDtypeStruct(out_grad.shape, BF16),
+            jax.ShapeDtypeStruct(grad.shape, F32),
+        ),
+        in_specs=[point, point, mode],
+        out_specs=(point, mode),
+        compiler_params=pltpu.CompilerParams(vmem_limit_bytes=LIMIT),
+        name="results",
+    )(out_grad, part, grad)
 
 
 def longitude_tables(lon_total):
@@ -778,7 +825,7 @@
             jax.ShapeDtypeStruct((KEEP, 2, CH // BS, BS * BS), F32),
         ),
         in_specs=[hbm] * 5 + [VMEM] + [hbm] * 6,
-        out_specs=(VMEM, VMEM),
+        out_specs=(hbm, hbm),
         scratch_shapes=kernel_scratch(),
         compiler_params=pltpu.CompilerParams(
             collective_id=0, has_side_effects=True, vmem_limit_bytes=LIMIT
@@ -794,9 +841,15 @@
         *longitude_tables(lon_total),
         *latitude_tables(lat_total),
     )
-    part = jnp.swapaxes(spectral_part, 0, 1)
-    input_grad = (out_grad.astype(F32) + part.astype(F32)).astype(BF16)
-    return input_grad, spectral_grad
+    input_grad, spectral_grad = result_call(
+        jnp.swapaxes(out_grad, 0, 1).reshape(LONS * ROWS, CH),
+        spectral_part.reshape(LONS * ROWS, CH),
+        spectral_grad.reshape(2 * KEEP * CH // BS, BS * BS),
+    )
+    return (
+        jnp.swapaxes(input_grad.reshape(LONS, ROWS, CH), 0, 1),
+        spectral_grad.reshape(KEEP, 2, CH // BS, BS * BS),
+    )
 
 
 def solution(mesh):

time: 131 us -> 130 us (level)
  other arithmetic: 3.2 us -> 0 us
  Pallas kernels: 125 us -> 128 us
    pallas_call x0 -> x1, Pallas kernels: none -> 4.18 us  [result_call(): pl.pallas_call(result_kernel, grid=(blocks,), out_shape=(jax.ShapeDtypeSt...]
    convert_element_type x1 -> x0, other arithmetic: 3.2 us -> none  [body(): input_grad = (out_grad.astype(F32) + part.astype(F32)).astype(BF16)]
    pallas_call x1, Pallas kernels: 125 us -> 124 us  [body(): pl.pallas_call(functools.partial(kernel, fwd_scale, syn_scale), out_shape...]
where the time goes in v4:
time: 130 us; the launch traced here: 129 us
  Pallas kernels  128 us (98%)
    pallas_call x1, Pallas kernels, body(): pl.pallas_call(functools.partial(kernel, fwd_scale, syn_scale), out_shape...  124 us
    pallas_call x1, Pallas kernels, result_call(): pl.pallas_call(result_kernel, grid=(blocks,), out_shape=(jax.ShapeDtypeSt...  4.18 us

profile of v4, /device:TPU:0, one launch (start us, length us, event | category | flops | bytes accessed | tf_op | source)
XLA Modules:
  0.0 128.7 jit_solution(9072111218185382179)
XLA Ops:
  0.6 123.9 %layer_gradients.1 = (bf16[45,64,256]{2,1,0:T(8,128)(2,1)}, f32[32,2,16,256]{3,2,1,0:T(8,128)}) custom-call(bf16[45,64,256]{2,1,0:T(8,128)(2,1)} %bitcast.13, bf16[45,64,256]{2,1,0:T(8,128)(2,1)} %bitcast.11, bf16[32,2,16,256]{3,2,1,0:T(8,128)(2,1)} %refs_2_.1, bf16[256,1024]{1,0:T(8,128)(2,1)} %refs_3_.1, bf16[1024,256]{1,0:T(8,128)(2,1)} %refs_4_.1, ...), custom_call_target="tpu_custom_call" | custom-call | tf_op jit(solution)/shard_map/layer_gradients/pallas_call | solution.py:821
  124.5 4.2 %results.1 = (bf16[2880,256]{1,0:T(8,128)(2,1)}, f32[1024,256]{1,0:T(8,128)}) custom-call(bf16[2880,256]{1,0:T(8,128)(2,1)} %bitcast.12, bf16[2880,256]{1,0:T(8,128)(2,1)} %bitcast.14, f32[1024,256]{1,0:T(8,128)} %bitcast.15), custom_call_target="tpu_custom_call" | custom-call | tf_op jit(solution)/shard_map/results/pallas_call | solution.py:768

commit v5 on v4

--- a/solution.py
+++ b/solution.py
@@ -18,9 +18,10 @@
 LONS_PAD = 48
 LON_BLOCKS = 32
 KEEP = 32
+ORDERS = (("xyz", "yzx"), ("yzx", "zxy"), ("zxy", "xyz"))
 HALVES = (
-    ((32, "xyz"), (16, "yzx"), (16, "zxy")),
-    ((32, "yzx"), (16, "xyz"), (16, "zxy")),
+    ((32, ORDERS[0]), (16, ORDERS[1]), (16, ORDERS[2])),
+    ((32, ORDERS[1]), (16, ORDERS[2]), (16, ORDERS[0])),
 )
 HALF = 128
 STRIDE = 72
@@ -28,7 +29,7 @@
 F32, BF16 = jnp.float32, jnp.bfloat16
 VMEM = pl.BlockSpec(memory_space=pltpu.VMEM)
 LIMIT = 60 << 20
-U_FILL, U_ROW, U_BLK, U_BUILD, GROUP, CHUNK, WORK = 5, 16, 8, 4, 9, 256, 3
+U_FILL, U_ROW, U_BLK, U_BUILD, GROUP, CHUNK, WORK = 5, 16, 8, 4, 9, 256, 2
 
 
 def matmul(a, b, contract=(1, 0)):
@@ -90,62 +91,94 @@
     return index
 
 
-def pair_of_sems(*shape):
-    return [pltpu.SemaphoreType.DMA(shape)] * 2
+def by_core(core, values):
+    return values[0] + (values[1] - values[0]) * core
+
+
+def piece_index(at, core, orders, depth=3):
+    return by_core(core, [index_of(at, order[:depth]) for order in orders])
+
+
+def along(at, orders, depth, step):
+    moves = [moved(at, order[depth], step) for order in orders]
+    there = {name: by_core(at["core"], [move[name] for move in moves]) for name in "xyz"}
+    return {**there, "core": at["core"]}
+
+
+def wait_bytes(ref, sem):
+    pltpu.make_async_copy(ref, ref, sem).wait()
+
+
+def dma(*shape):
+    return pltpu.SemaphoreType.DMA(shape)
+
+
+def gather_sems():
+    return [dma(3), dma(3, 2), dma(3, 3), dma(3)]
 
 
 def gather(at, pieces, full, sems):
-    ring_send, ring_recv, core_send, core_recv = sems
-    bases = [at["core"] * (64 * size) for size, _ in pieces]
+    sent, recv, far_recv, core_recv = sems
+    core = at["core"]
     sibling = moved(at, "core", 1)
-    pending, across = [], []
-    sent = [[] for _ in pieces]
-
-    def across_core(i, s, step):
-        size, order = pieces[i]
-        slab = lax.rem(at[order[0]] + step, RING)
-        here = full[i].at[rows(bases[i] + slab * (16 * size), 16 * size)]
-        across.append(send(here, here, (core_send.at[i, s], core_recv.at[i, s]), sibling))
-
-    for phase in range(3):
-        for i, (size, order) in enumerate(pieces):
-            for copy in sent[i]:
-                copy.wait_recv()
+
+    def slab(i, step, first, count):
+        size, orders = pieces[i]
+        place = lax.rem(piece_index(at, core, orders, 1) + step, RING)
+        start = core * (64 * size) + place * (16 * size) + first * (8 * size)
+        return full[i].at[rows(start, count * (8 * size))]
+
+    def give(i, here, sem, target):
+        send(here, here, (sent.at[i], sem), target)
+
+    for phase in range(2):
+        for i in (1, 2, 0):
+            size, orders = pieces[i]
+            if phase:
+                wait_bytes(full[i].at[0 : 3 * size], recv.at[i, 0])
             block = size * RING**phase
-            index = index_of(at, order[: 3 - phase])
-            here = full[i].at[rows(bases[i] + index * block, block)]
-            sent[i] = [
-                send(
-                    here,
-                    here,
-                    (ring_send.at[i, phase, s], ring_recv.at[i, phase, s]),
-                    moved(at, order[2 - phase], step),
-                )
-                for s, step in enumerate(STEPS)
-            ]
-            pending += sent[i]
-        if phase == 2:
-            for i in range(len(pieces)):
-                across_core(i, 0, 0)
+            index = piece_index(at, core, orders, 3 - phase)
+            here = full[i].at[rows(core * (64 * size) + index * block, block)]
+            for step in STEPS:
+                give(i, here, recv.at[i, phase], along(at, orders, 2 - phase, step))
         yield
-    for s in (1, 2, 0):
-        for i in range(len(pieces)):
-            sent[i][s].wait_recv()
-            across_core(i, s + 1, RING - STEPS[s])
+    for i in (1, 2, 0):
+        size, orders = pieces[i]
+        wait_bytes(full[i].at[0 : 12 * size], recv.at[i, 1])
+        right, left = along(at, orders, 0, 1), along(at, orders, 0, 3)
+        give(i, slab(i, 0, 0, 1), far_recv.at[i, 0], right)
+        give(i, slab(i, 0, 1, 1), far_recv.at[i, 0], left)
+        give(i, slab(i, 0, 1, 1), far_recv.at[i, 1], right)
+        give(i, slab(i, 0, 0, 1), far_recv.at[i, 1], left)
+    for i in range(3):
+        give(i, slab(i, 0, 0, 2), core_recv.at[i], sibling)
     yield
-    for copy in across:
-        copy.wait_recv()
-    for copy in pending + across:
-        copy.wait_send()
+    for i in (1, 2, 0):
+        size, orders = pieces[i]
+        wait_bytes(full[i].at[0 : 16 * size], far_recv.at[i, 0])
+        give(i, slab(i, 3, 0, 1), far_recv.at[i, 2], along(at, orders, 0, 1))
+        give(i, slab(i, 1, 1, 1), far_recv.at[i, 2], along(at, orders, 0, 3))
+    yield
+    for kind, steps in ((1, (1, 3)), (2, (2,))):
+        for i in (1, 2, 0):
+            size, _ = pieces[i]
+            wait_bytes(full[i].at[0 : 16 * size], far_recv.at[i, kind])
+            for step in steps:
+                give(i, slab(i, step, 0, 2), core_recv.at[i], sibling)
+    yield
+    for i, (size, _) in enumerate(pieces):
+        wait_bytes(full[i].at[0 : 64 * size], core_recv.at[i])
+        wait_bytes(full[i].at[0 : 127 * size], sent.at[i])
 
 
 def scatter_scratch(pieces):
-    scratch = [*pair_of_sems(3, 3, 3), *pair_of_sems(3, 4)]
+    scratch = [dma(3), dma(3, 4), dma(3, 4)]
     for size, _ in pieces:
         scratch += [
             pltpu.VMEM((64 * size, HALF), BF16),
             pltpu.VMEM((64 * size, HALF), BF16),
-            pltpu.VMEM((3, 16 * size, HALF), BF16),
+            pltpu.VMEM((2, 8 * size, HALF), BF16),
+            pltpu.VMEM((2, 16 * size, HALF), BF16),
             pltpu.VMEM((16 * size, HALF), BF16),
             pltpu.VMEM((3, 4 * size, HALF), BF16),
             pltpu.VMEM((4 * size, HALF), BF16),
@@ -155,76 +188,94 @@
 
 
 def reduce_scatter(at, pieces, parts, scale, out, scratch):
-    ring_send, ring_recv, core_send, core_recv = scratch[:4]
-    bufs = [scratch[4 + 7 * i : 11 + 7 * i] for i in range(3)]
+    sent, core_recv, recv = scratch[:3]
+    bufs = [scratch[3 + 8 * i : 11 + 8 * i] for i in range(3)]
+    core = at["core"]
     sibling = moved(at, "core", 1)
-    pending, across = [], {}
-    for s, step in enumerate(STEPS + (0,)):
-        for i, (size, order) in enumerate(pieces):
-            slab = lax.rem(at[order[0]] + step, RING) * (16 * size)
-            across[s, i] = send(
-                parts[i].at[rows((1 - at["core"]) * (64 * size) + slab, 16 * size)],
-                bufs[i][0].at[rows(slab, 16 * size)],
-                (core_send.at[i, s], core_recv.at[i, s]),
+
+    def slab(i, owner, step):
+        size, orders = pieces[i]
+        return lax.rem(piece_index(at, owner, orders, 1) + step, RING) * (16 * size)
+
+    for s, step in enumerate((2, 1, 3, 0)):
+        for i, (size, orders) in enumerate(pieces):
+            start = slab(i, 1 - core, step)
+            send(
+                parts[i].at[rows((1 - core) * (64 * size) + start, 16 * size)],
+                bufs[i][0].at[rows(start, 16 * size)],
+                (sent.at[i], core_recv.at[i, s]),
                 sibling,
             )
     yield
-    sent = [[], [], []]
-    for s, step in enumerate(STEPS + (0,)):
-        for i, (size, order) in enumerate(pieces):
-            slab = lax.rem(at[order[0]] + step, RING) * (16 * size)
-            across[s, i].wait_recv()
-            here = rows(slab, 16 * size)
-            own = parts[i][rows(at["core"] * (64 * size) + slab, 16 * size), :]
-            bufs[i][1][here, :] = (own.astype(F32) + bufs[i][0][here, :].astype(F32)).astype(BF16)
-            if step:
-                sent[i].append(
-                    send(
-                        bufs[i][1].at[here],
-                        bufs[i][2].at[s],
-                        (ring_send.at[i, 0, s], ring_recv.at[i, 0, s]),
-                        moved(at, order[0], step),
-                    )
-                )
+
+    def give(i, step, first, kind, dst, target):
+        size, _ = pieces[i]
+        here = rows(slab(i, core, step) + first * (8 * size), 8 * size)
+        send(bufs[i][1].at[here], dst, (sent.at[i], recv.at[i, kind]), target)
+
+    for s, step in enumerate((2, 1, 3, 0)):
+        for i, (size, orders) in enumerate(pieces):
+            sib, total, onward, landed = bufs[i][:4]
+            right, left = along(at, orders, 0, 1), along(at, orders, 0, 3)
+            start = slab(i, core, step)
+            here = rows(start, 16 * size)
+            wait_bytes(sib.at[here], core_recv.at[i, s])
+            mine = parts[i][rows(core * (64 * size) + start, 16 * size), :]
+            total[here, :] = (mine.astype(F32) + sib[here, :].astype(F32)).astype(BF16)
+            if step == 2:
+                give(i, 2, 0, 0, onward.at[0], right)
+                give(i, 2, 1, 0, onward.at[1], left)
+            elif step == 1:
+                give(i, 1, 1, 1, landed.at[0, 8 * size : 16 * size], right)
+            elif step == 3:
+                give(i, 3, 0, 1, landed.at[1, 0 : 8 * size], left)
     yield
-    first = 0
+    for i in (1, 2, 0):
+        size, orders = pieces[i]
+        _, total, onward, landed = bufs[i][:4]
+        wait_bytes(onward, recv.at[i, 0])
+        for way, (step, first) in enumerate(((1, 0), (3, 1))):
+            here = rows(slab(i, core, step) + first * (8 * size), 8 * size)
+            total[here, :] = (total[here, :].astype(F32) + onward[way].astype(F32)).astype(BF16)
+            dst = landed.at[way, first * (8 * size) : (first + 1) * (8 * size)]
+            give(i, step, first, 1, dst, along(at, orders, 0, step))
+    yield
     for phase in range(3):
-        first = 0
-        for i, (size, order) in enumerate(pieces):
+        for i in (1, 2, 0):
+            size, orders = pieces[i]
+            mine, landed = ((1, 3), (4, 5), (6, 7))[phase]
+            mine, landed = bufs[i][mine], bufs[i][landed]
             block = size * RING ** (2 - phase)
-            mine, landed = bufs[i][1 + 2 * phase], bufs[i][2 + 2 * phase]
-            total = mine[rows(at[order[phase]] * block, block), :].astype(F32)
-            for s in (1, 2, 0):
-                sent[i][s].wait_recv()
+            place = by_core(core, [at[order[phase]] for order in orders])
+            total = mine[rows(place * block, block), :].astype(F32)
+            wait_bytes(landed, recv.at[i, phase + 1])
+            for s in range(landed.shape[0]):
                 total = total + landed[s].astype(F32)
-            pending += sent[i]
             if phase == 2:
+                first = sum(before for before, _ in pieces[:i])
                 out[first : first + size, :] = total * scale
-                first += size
                 continue
-            after = bufs[i][3 + 2 * phase]
+            after, there = bufs[i][4 + 2 * phase], bufs[i][5 + 2 * phase]
             after[...] = total.astype(BF16)
             small = block // RING
-            axis = order[phase + 1]
-            sent[i] = [
+            place = by_core(core, [at[order[phase + 1]] for order in orders])
+            for s, step in enumerate(STEPS):
                 send(
-                    after.at[rows(lax.rem(at[axis] + step, RING) * small, small)],
-                    bufs[i][4 + 2 * phase].at[s],
-                    (ring_send.at[i, phase + 1, s], ring_recv.at[i, phase + 1, s]),
-                    moved(at, axis, step),
+                    after.at[rows(lax.rem(place + step, RING) * small, small)],
+                    there.at[s],
+                    (sent.at[i], recv.at[i, phase + 2]),
+                    along(at, orders, phase + 1, step),
                 )
-                for s, step in enumerate(STEPS)
-            ]
         if phase < 2:
             yield
-    for copy in pending + list(across.values()):
-        copy.wait_send()
+    for i, (size, _) in enumerate(pieces):
+        wait_bytes(parts[i].at[0 : 127 * size], sent.at[i])
 
 
 def put_own(at, pieces, modes, full):
     first = 0
-    for i, (size, order) in enumerate(pieces):
-        here = rows((at["core"] * 64 + index_of(at, order)) * size, size)
+    for i, (size, orders) in enumerate(pieces):
+        here = rows((at["core"] * 64 + piece_index(at, at["core"], orders)) * size, size)
         full[i][here, :] = modes[first : first + size]
         first += size
 
@@ -239,43 +290,31 @@
 
 
 def gather_slots(at, own, other, full, sems):
-    core_send, core_recv, line_send, line_recv, plane_send, plane_recv, past = sems
-    copies = [send(own, other, (core_send.at[0], core_recv.at[0]), moved(at, "core", 1))]
+    sems, past = sems
+    copy = send(own, other, (sems.at[0], sems.at[1]), moved(at, "core", 1))
     for step in STEPS:
         pl.semaphore_signal(
             past, inc=1, device_id=device_of(moved(at, "y", step)), device_id_type=MESH
         )
-    copies[0].wait_recv()
+    copy.wait_recv()
     mine = rows(index_of(at, "yzx") * 8, 8)
     full[mine, :] = own[...] + other[...]
-    line = [
-        send(full.at[mine], full.at[mine], (line_send.at[s], line_recv.at[s]), moved(at, "x", step))
-        for s, step in enumerate(STEPS)
-    ]
+    for step in STEPS:
+        send(full.at[mine], full.at[mine], (sems.at[2], sems.at[3]), moved(at, "x", step))
     yield
-    for copy in line:
-        copy.wait_recv()
+    wait_bytes(full.at[0:24], sems.at[3])
     pl.semaphore_wait(past, len(STEPS))
     here = full.at[rows(index_of(at, "yz") * 32, 32)]
-    plane = []
-    for dy, dz in ((2, 2), (2, 1), (2, 3), (1, 2), (3, 2), (1, 1), (1, 3), (3, 1), (3, 3)):
-        plane.append((dy, dz))
+    ways = [(dy, dz) for dy in STEPS for dz in STEPS]
     for step in STEPS:
-        plane += [(step, 0), (0, step)]
-    plane = [
-        send(
-            here,
-            here,
-            (plane_send.at[dy, dz], plane_recv.at[dy, dz]),
-            moved(moved(at, "y", dy), "z", dz),
-        )
-        for dy, dz in plane
-    ]
+        ways += [(step, 0), (0, step)]
+    for dy, dz in ways:
+        send(here, here, (sems.at[4], sems.at[5]), moved(moved(at, "y", dy), "z", dz))
     yield
-    for copy in plane:
-        copy.wait_recv()
-    for copy in copies + line + plane:
-        copy.wait_send()
+    wait_bytes(full.at[0:480], sems.at[5])
+    copy.wait_send()
+    wait_bytes(full.at[0:24], sems.at[2])
+    wait_bytes(full.at[0:480], sems.at[4])
 
 
 def collect_slots(full, slots):
@@ -286,7 +325,8 @@
         slots[b : b + 1, :] = total[0:1]
 
 
-def piece_start(b, lat, size, order):
+def piece_start(b, lat, size, orders):
+    order = orders[lat % 2]
     place = {"x": lax.div(b, 8), "z": lax.rem(lax.div(b, 4), 2) * 2 + lat // 2, "y": lax.rem(b, 4)}
     return rows((lat % 2 * 64 + index_of(place, order)) * size, size)
 
@@ -586,9 +626,9 @@
     parts, full = [take(3), take(3)], [take(3), take(3)]
     tables, hidden, slots, own, other, slots_full = take(6)
     modes, weights, wide_in, wide_grad = take(2), take(2), take(2), take(2)
-    slot_sems = take(7)
+    slot_sems = take(2)
     gather_sems = [take(4), take(4)]
-    scatter = [take(25), take(25)]
+    scatter = [take(27), take(27)]
     analysis, synthesis = tables.at[0:8192], tables.at[8192:16384]
 
     at = own_place()
@@ -660,7 +700,7 @@
         next(first)
         before()
         next(second)
-        for _ in range(6):
+        for _ in range(8):
             for task in work[:WORK]:
                 task()
             del work[:WORK]
@@ -701,6 +741,7 @@
             )
         )
         work += [lambda: None] * (WORK - 1)
+    work += [lambda: None] * WORK
     for h in range(2):
         work.append(
             functools.partial(weight_gradient, h, wide_in[h], wide_grad[h], spectral_grad)
@@ -731,8 +772,8 @@
         v((2, 2 * KLAT, 2 * ROWS), BF16),
         v((2, 2 * ROWS, 2 * KLAT), BF16),
         v((2, 2 * ROWS, 2 * KLAT), BF16),
-        pltpu.SemaphoreType.DMA((11,)),
-        pltpu.SemaphoreType.DMA((3,)),
+        dma(11),
+        dma(3),
         v((KEEP, 2, CH // BS, BS * BS), F32),
         *[v((LONS_PAD * STRIDE, HALF), F32)] * 2,
         *[v((2 * KM * STRIDE, HALF), F32)] * 2,
@@ -746,11 +787,10 @@
         v((512, 128), F32),
         *[v((2 * KEEP, HALF), F32)] * 2,
         *[v((2 * KEEP * BETAS, CH), F32)] * 6,
-        *pair_of_sems(1),
-        *pair_of_sems(3),
-        *pair_of_sems(4, 4),
+        dma(6),
         pltpu.SemaphoreType.REGULAR,
-        *[*pair_of_sems(3, 3, 3), *pair_of_sems(3, 4)] * 2,
+        *gather_sems(),
+        *gather_sems(),
         *scatter_scratch(HALVES[0]),
         *scatter_scratch(HALVES[1]),
     ]

time: 130 us -> 124 us (0.954)
  Pallas kernels: 128 us -> 123 us
    pallas_call x1, Pallas kernels: 124 us -> 118 us  [body(): pl.pallas_call(functools.partial(kernel, fwd_scale, syn_scale), out_shape...]
where the time goes in v5:
time: 124 us; the launch traced here: 123 us
  Pallas kernels  123 us (99%)
    pallas_call x1, Pallas kernels, body(): pl.pallas_call(functools.partial(kernel, fwd_scale, syn_scale), out_shape...  118 us
    pallas_call x1, Pallas kernels, result_call(): pl.pallas_call(result_kernel, grid=(blocks,), out_shape=(jax.ShapeDtypeSt...  4.18 us

profile of v5, /device:TPU:0, one launch (start us, length us, event | category | flops | bytes accessed | tf_op | source)
XLA Modules:
  0.0 123.2 jit_solution(18149941060000233574)
XLA Ops:
  0.6 118.3 %layer_gradients.1 = (bf16[45,64,256]{2,1,0:T(8,128)(2,1)}, f32[32,2,16,256]{3,2,1,0:T(8,128)}) custom-call(bf16[45,64,256]{2,1,0:T(8,128)(2,1)} %bitcast.13, bf16[45,64,256]{2,1,0:T(8,128)(2,1)} %bitcast.11, bf16[32,2,16,256]{3,2,1,0:T(8,128)(2,1)} %refs_2_.1, bf16[256,1024]{1,0:T(8,128)(2,1)} %refs_3_.1, bf16[1024,256]{1,0:T(8,128)(2,1)} %refs_4_.1, ...), custom_call_target="tpu_custom_call" | custom-call | tf_op jit(solution)/shard_map/layer_gradients/pallas_call | solution.py:861
  119.0 4.2 %results.1 = (bf16[2880,256]{1,0:T(8,128)(2,1)}, f32[1024,256]{1,0:T(8,128)}) custom-call(bf16[2880,256]{1,0:T(8,128)(2,1)} %bitcast.12, bf16[2880,256]{1,0:T(8,128)(2,1)} %bitcast.14, f32[1024,256]{1,0:T(8,128)} %bitcast.15), custom_call_target="tpu_custom_call" | custom-call | tf_op jit(solution)/shard_map/results/pallas_call | solution.py:808

commit v6 on v5

--- a/solution.py
+++ b/solution.py
@@ -29,7 +29,7 @@
 F32, BF16 = jnp.float32, jnp.bfloat16
 VMEM = pl.BlockSpec(memory_space=pltpu.VMEM)
 LIMIT = 60 << 20
-U_FILL, U_ROW, U_BLK, U_BUILD, GROUP, CHUNK, WORK = 5, 16, 8, 4, 9, 256, 2
+U_FILL, U_ROW, U_BLK, U_BUILD, GROUP, CHUNK = 5, 16, 8, 4, 9, 256
 
 
 def matmul(a, b, contract=(1, 0)):
@@ -221,7 +221,7 @@
             here = rows(start, 16 * size)
             wait_bytes(sib.at[here], core_recv.at[i, s])
             mine = parts[i][rows(core * (64 * size) + start, 16 * size), :]
-            total[here, :] = (mine.astype(F32) + sib[here, :].astype(F32)).astype(BF16)
+            total[here, :] = mine + sib[here, :]
             if step == 2:
                 give(i, 2, 0, 0, onward.at[0], right)
                 give(i, 2, 1, 0, onward.at[1], left)
@@ -236,7 +236,7 @@
         wait_bytes(onward, recv.at[i, 0])
         for way, (step, first) in enumerate(((1, 0), (3, 1))):
             here = rows(slab(i, core, step) + first * (8 * size), 8 * size)
-            total[here, :] = (total[here, :].astype(F32) + onward[way].astype(F32)).astype(BF16)
+            total[here, :] = total[here, :] + onward[way]
             dst = landed.at[way, first * (8 * size) : (first + 1) * (8 * size)]
             give(i, step, first, 1, dst, along(at, orders, 0, step))
     yield
@@ -491,10 +491,11 @@
 
 def gelu_slope(x):
     c, a = math.sqrt(2.0 / math.pi), 0.044715
-    square = x * x
-    t = jnp.tanh(x * (c + (c * a) * square))
-    half = 0.5 + 0.5 * t
-    return half + x * (half * (1.0 - t)) * (c + (3.0 * c * a) * square)
+    cubic = (x * x) * jnp.asarray(c * a, x.dtype)
+    linear = cubic + jnp.asarray(c, x.dtype)
+    one = jnp.asarray(1.0, x.dtype)
+    t = jnp.tanh(x * linear)
+    return (one + t) * (one + (one - t) * (x * (linear + (cubic + cubic))))
 
 
 def hidden_gradient(out_grad, w2, hidden, low, high):
@@ -503,7 +504,7 @@
         here = pl.ds(pl.multiple_of(i * (GROUP * ROWS), GROUP * ROWS), GROUP * ROWS)
         for k in range(HID // CHUNK):
             cols = slice(CHUNK * k, CHUNK * k + CHUNK)
-            hidden[here, cols] = matmul(grad, w2[cols, :], (1, 1)).astype(BF16)
+            hidden[here, cols] = (0.5 * matmul(grad, w2[cols, :], (1, 1))).astype(BF16)
         return carry
 
     lax.fori_loop(low, high, one, 0)
@@ -517,8 +518,8 @@
         total = None
         for k in range(HID // CHUNK):
             cols = slice(CHUNK * k, CHUNK * k + CHUNK)
-            pre = matmul(value, w1[:, cols])
-            pre_grad = (gelu_slope(pre) * hidden[here, cols].astype(F32)).astype(BF16)
+            pre = matmul(value, w1[:, cols]).astype(BF16)
+            pre_grad = gelu_slope(pre) * hidden[here, cols]
             term = matmul(pre_grad, w1[:, cols], (1, 1))
             total = term if total is None else total + term
         for j in range(GROUP):
@@ -700,30 +701,36 @@
         next(first)
         before()
         next(second)
-        for _ in range(8):
-            for task in work[:WORK]:
+        for tasks in work:
+            for task in tasks:
                 task()
-            del work[:WORK]
             next(first)
             next(second)
-        for task in work:
-            task()
         next(first)
         next(first, None)
         next(second)
         next(second, None)
 
     quarter = LON_BLOCKS // 4
-    work = [lambda: [copy.wait() for copy in loads[3:]]]
+    tasks = []
     for low in range(0, LON_BLOCKS, quarter):
         span = (low, low + quarter)
-        work += [
+        tasks += [
             functools.partial(build_analysis, slots, plain, analysis, *span),
             functools.partial(build_synthesis, slots, plain_back, synthesis, *span),
         ]
-    work.insert(1, functools.partial(widen_weight, weight, weights))
     for i in range(LONS // GROUP):
-        work.append(functools.partial(hidden_gradient, out_grad, w2, hidden, i, i + 1))
+        tasks.append(functools.partial(hidden_gradient, out_grad, w2, hidden, i, i + 1))
+
+    def prepare():
+        for copy in loads[3:]:
+            copy.wait()
+        widen_weight(weight, weights)
+
+    work = [[prepare]]
+    for count in (3, 2, 2, 1, 2, 1, 2):
+        work.append(tasks[:count])
+        del tasks[:count]
     drive(*[exchange(h, fwd_scale, False, syn_scale) for h in range(2)], work)
 
     pointwise(points, hidden, w1, 0, LONS // GROUP)
@@ -733,20 +740,16 @@
         analyse_latitude(rows_spec[h], analysis, HALVES[h], parts[h])
 
     analyse(0)
-    work = []
-    for low in range(0, LON_BLOCKS, quarter):
-        work.append(
-            functools.partial(
-                build_synthesis, slots, doubled_back, synthesis, low, low + quarter
-            )
-        )
-        work += [lambda: None] * (WORK - 1)
-    work += [lambda: None] * WORK
-    for h in range(2):
-        work.append(
-            functools.partial(weight_gradient, h, wide_in[h], wide_grad[h], spectral_grad)
-        )
-    work.append(lambda: store(spectral_grad, grad_hbm))
+    tables_back = [
+        functools.partial(build_synthesis, slots, doubled_back, synthesis, low, low + quarter)
+        for low in range(0, LON_BLOCKS, quarter)
+    ]
+    gradients = [
+        functools.partial(weight_gradient, h, wide_in[h], wide_grad[h], spectral_grad)
+        for h in range(2)
+    ]
+    work = [[], tables_back[:2], tables_back[2:], [], [], gradients[:1], gradients[1:]]
+    work.append([lambda: store(spectral_grad, grad_hbm)])
     drive(
         *[exchange(h, syn_scale, True, fwd_scale) for h in range(2)],
         work,
@@ -802,7 +805,7 @@
 
 
 def result_call(out_grad, part, grad):
-    blocks = 4
+    blocks = 2
     point = pl.BlockSpec((LONS * ROWS // blocks, CH), lambda i: (i, 0))
     mode = pl.BlockSpec((2 * KEEP * CH // BS // blocks, BS * BS), lambda i: (i, 0))
     return pl.pallas_call(

time: 124 us -> 120 us (0.968)
  Pallas kernels: 123 us -> 119 us
    pallas_call x1, Pallas kernels: 118 us -> 115 us  [body(): pl.pallas_call(functools.partial(kernel, fwd_scale, syn_scale), out_shape...]
where the time goes in v6:
time: 120 us; the launch traced here: 119 us
  Pallas kernels  119 us (99%)
    pallas_call x1, Pallas kernels, body(): pl.pallas_call(functools.partial(kernel, fwd_scale, syn_scale), out_shape...  115 us
    pallas_call x1, Pallas kernels, result_call(): pl.pallas_call(result_kernel, grid=(blocks,), out_shape=(jax.ShapeDtypeSt...  3.29 us

profile of v6, /device:TPU:0, one launch (start us, length us, event | category | flops | bytes accessed | tf_op | source)
XLA Modules:
  0.0 119.3 jit_solution(18089738218456420731)
XLA Ops:
  0.6 115.3 %layer_gradients.1 = (bf16[45,64,256]{2,1,0:T(8,128)(2,1)}, f32[32,2,16,256]{3,2,1,0:T(8,128)}) custom-call(bf16[45,64,256]{2,1,0:T(8,128)(2,1)} %bitcast.13, bf16[45,64,256]{2,1,0:T(8,128)(2,1)} %bitcast.11, bf16[32,2,16,256]{3,2,1,0:T(8,128)(2,1)} %refs_2_.1, bf16[256,1024]{1,0:T(8,128)(2,1)} %refs_3_.1, bf16[1024,256]{1,0:T(8,128)(2,1)} %refs_4_.1, ...), custom_call_target="tpu_custom_call" | custom-call | tf_op jit(solution)/shard_map/layer_gradients/pallas_call | solution.py:864
  116.0 3.3 %results.1 = (bf16[2880,256]{1,0:T(8,128)(2,1)}, f32[1024,256]{1,0:T(8,128)}) custom-call(bf16[2880,256]{1,0:T(8,128)(2,1)} %bitcast.12, bf16[2880,256]{1,0:T(8,128)(2,1)} %bitcast.14, f32[1024,256]{1,0:T(8,128)} %bitcast.15), custom_call_target="tpu_custom_call" | custom-call | tf_op jit(solution)/shard_map/results/pallas_call | solution.py:811

commit v7 on v6

--- a/solution.py
+++ b/solution.py
@@ -30,6 +30,7 @@
 VMEM = pl.BlockSpec(memory_space=pltpu.VMEM)
 LIMIT = 60 << 20
 U_FILL, U_ROW, U_BLK, U_BUILD, GROUP, CHUNK = 5, 16, 8, 4, 9, 256
+U_HALF_ROW, U_HALF_BLK = 64, 32
 
 
 def matmul(a, b, contract=(1, 0)):
@@ -168,7 +169,11 @@
     yield
     for i, (size, _) in enumerate(pieces):
         wait_bytes(full[i].at[0 : 64 * size], core_recv.at[i])
-        wait_bytes(full[i].at[0 : 127 * size], sent.at[i])
+
+
+def wait_sent(pieces, buffers, sent):
+    for i, (size, _) in enumerate(pieces):
+        wait_bytes(buffers[i].at[0 : 127 * size], sent.at[i])
 
 
 def scatter_scratch(pieces):
@@ -268,8 +273,6 @@
                 )
         if phase < 2:
             yield
-    for i, (size, _) in enumerate(pieces):
-        wait_bytes(parts[i].at[0 : 127 * size], sent.at[i])
 
 
 def put_own(at, pieces, modes, full):
@@ -284,12 +287,14 @@
     lat = lax.rem(at["z"], 2) * 2 + at["core"]
     value = jnp.concatenate([kept[...]] * 4, axis=1)
     slot = (value & 1) * KLAT + lat * KEEP + lax.shift_right_logical(value, 1)
-    lane = lax.broadcasted_iota(jnp.int32, (1, 128), 1)
-    own = jnp.where(lax.shift_right_logical(lane, 5) == lat, slot.astype(F32), 0.0)
-    return jnp.broadcast_to(own, (8, 128))
-
-
-def gather_slots(at, own, other, full, sems):
+    slot = jnp.broadcast_to(slot.astype(F32), (8, 128))
+    lane = lax.broadcasted_iota(jnp.int32, (8, 128), 1)
+    row = lax.broadcasted_iota(jnp.int32, (8, 128), 0)
+    here = (lax.shift_right_logical(lane, 5) == lat) & (row == at["x"])
+    return jnp.where(here, slot, 0.0)
+
+
+def gather_slots(at, own, other, line, full, sems):
     sems, past = sems
     copy = send(own, other, (sems.at[0], sems.at[1]), moved(at, "core", 1))
     for step in STEPS:
@@ -297,32 +302,33 @@
             past, inc=1, device_id=device_of(moved(at, "y", step)), device_id_type=MESH
         )
     copy.wait_recv()
-    mine = rows(index_of(at, "yzx") * 8, 8)
-    full[mine, :] = own[...] + other[...]
-    for step in STEPS:
-        send(full.at[mine], full.at[mine], (sems.at[2], sems.at[3]), moved(at, "x", step))
+    mine = full.at[rows(index_of(at, "yz") * 8, 8)]
+    both_cores = own[...] + other[...]
+    line[3] = both_cores
+    for s, step in enumerate(STEPS):
+        send(line.at[3], line.at[s], (sems.at[2], sems.at[3]), moved(at, "x", step))
     yield
-    wait_bytes(full.at[0:24], sems.at[3])
+    wait_bytes(line.at[0:3], sems.at[3])
     pl.semaphore_wait(past, len(STEPS))
-    here = full.at[rows(index_of(at, "yz") * 32, 32)]
+    mine[...] = (line[0] + line[1]) + (line[2] + line[3])
     ways = [(dy, dz) for dy in STEPS for dz in STEPS]
     for step in STEPS:
         ways += [(step, 0), (0, step)]
     for dy, dz in ways:
-        send(here, here, (sems.at[4], sems.at[5]), moved(moved(at, "y", dy), "z", dz))
+        send(mine, mine, (sems.at[4], sems.at[5]), moved(moved(at, "y", dy), "z", dz))
     yield
-    wait_bytes(full.at[0:480], sems.at[5])
+    wait_bytes(full.at[0:120], sems.at[5])
+    yield
     copy.wait_send()
-    wait_bytes(full.at[0:24], sems.at[2])
-    wait_bytes(full.at[0:480], sems.at[4])
+    wait_bytes(line.at[0:3], sems.at[2])
+    wait_bytes(full.at[0:120], sems.at[4])
 
 
 def collect_slots(full, slots):
     for b in range(LON_BLOCKS):
         x, zhi, y = b // 8, b // 4 % 2, b % 4
-        first = ((y * 4 + zhi * 2) * 4 + x) * 8
-        total = full[first : first + 8, :] + full[first + 32 : first + 40, :]
-        slots[b : b + 1, :] = total[0:1]
+        first = (y * 4 + zhi * 2) * 8 + x
+        slots[b : b + 1, :] = full[first : first + 1, :] + full[first + 8 : first + 9, :]
 
 
 def piece_start(b, lat, size, orders):
@@ -372,7 +378,7 @@
             half[pl.ds(g, 2 * KM, stride=STRIDE), :] = spec[:, HALF * h : HALF * h + HALF]
         return carry
 
-    lax.fori_loop(0, ROWS, one, 0, unroll=U_ROW)
+    lax.fori_loop(0, ROWS, one, 0, unroll=U_ROW if len(rows_spec) == 2 else U_HALF_ROW)
 
 
 def synthesise_longitude(rows_spec, basis_back, points, scale):
@@ -381,7 +387,7 @@
         points[pl.ds(g, LONS_PAD, stride=STRIDE), :] = matmul(basis_back[...], spec) * scale
         return carry
 
-    lax.fori_loop(0, ROWS, one, 0, unroll=U_ROW)
+    lax.fori_loop(0, ROWS, one, 0, unroll=U_HALF_ROW)
 
 
 def spec_block(b, size=256):
@@ -476,7 +482,7 @@
             store_modes(b, part, modes[128 * part : 128 * part + 128], pieces, parts)
         return carry
 
-    lax.fori_loop(0, LON_BLOCKS, one, 0, unroll=U_BLK)
+    lax.fori_loop(0, LON_BLOCKS, one, 0, unroll=U_HALF_BLK)
 
 
 def synthesise_latitude(pieces, full, table, rows_spec):
@@ -486,7 +492,7 @@
             rows_spec[group(b * 4 + q), :] = value[ROWS * q : ROWS * q + ROWS]
         return carry
 
-    lax.fori_loop(0, LON_BLOCKS, one, 0, unroll=U_BLK)
+    lax.fori_loop(0, LON_BLOCKS, one, 0, unroll=U_HALF_BLK)
 
 
 def gelu_slope(x):
@@ -550,12 +556,6 @@
     return jnp.where(beta == lax.shift_right_logical(channel, 4), 1.0, 0.0)[None]
 
 
-def exact(value, ones):
-    high = value.astype(BF16)
-    low = (value - high.astype(F32)).astype(BF16)
-    return matmul(high, ones) + matmul(low, ones)
-
-
 def widen_weight(weight, wide):
     def one(e, carry):
         for part in range(2):
@@ -573,7 +573,7 @@
     for i in range(2 * KEEP // MIX):
         value = modes[MIX * i : MIX * i + MIX, :]
         wide = (value[:, None, :] * mask).reshape(MIX * BETAS, HALF)
-        out[MIX * BETAS * i : MIX * BETAS * (i + 1), :] = exact(wide, match)
+        out[MIX * BETAS * i : MIX * BETAS * (i + 1), :] = matmul(wide.astype(BF16), match)
 
 
 def mixing_rows(i):
@@ -594,7 +594,7 @@
         else:
             terms = re * wr - im * wi, re * wi + im * wr
         for part, term in enumerate(terms):
-            total = exact(term, sums).reshape(MIX, BETAS, HALF) * mask
+            total = matmul(term.astype(BF16), sums).reshape(MIX, BETAS, HALF) * mask
             out[part].append(jnp.sum(total, axis=1))
     return jnp.concatenate(out[0] + out[1], axis=0).astype(BF16)
 
@@ -625,7 +625,7 @@
     (spectral_grad,) = take(1)
     points, rows_spec = take(2), take(2)
     parts, full = [take(3), take(3)], [take(3), take(3)]
-    tables, hidden, slots, own, other, slots_full = take(6)
+    tables, hidden, slots, own, other, slots_line, slots_full = take(7)
     modes, weights, wide_in, wide_grad = take(2), take(2), take(2), take(2)
     slot_sems = take(2)
     gather_sems = [take(4), take(4)]
@@ -659,14 +659,14 @@
     fill_points(field, points)
     pl.semaphore_wait(pltpu.get_barrier_semaphore(), greeted)
 
-    collecting = gather_slots(at, own, other, slots_full, slot_sems)
+    collecting = gather_slots(at, own, other, slots_line, slots_full, slot_sems)
     next(collecting)
     loads[1].wait()
     analyse_longitude(points, basis, rows_spec)
     next(collecting)
     loads[2].wait()
     analyse_dense(rows_spec, doubled, tables)
-    next(collecting, None)
+    next(collecting)
     collect_slots(slots_full, slots)
     select_modes(tables, slots, parts)
 
@@ -692,8 +692,10 @@
         spread(modes[h], not backward, wide)
         put_own(at, HALVES[h], mix(wide, weights[h], backward), full[h])
         yield from gather(at, HALVES[h], full[h], gather_sems[h])
+        wait_sent(HALVES[h], parts[h], scatter[h][0])
         synthesise_latitude(HALVES[h], full[h], synthesis, rows_spec[h])
         synthesise_longitude(rows_spec[h], basis_back, points[h], synthesised)
+        wait_sent(HALVES[h], full[h], gather_sems[h][0])
         if backward:
             finish(h)
 
@@ -723,6 +725,7 @@
         tasks.append(functools.partial(hidden_gradient, out_grad, w2, hidden, i, i + 1))
 
     def prepare():
+        next(collecting, None)
         for copy in loads[3:]:
             copy.wait()
         widen_weight(weight, weights)
@@ -787,7 +790,8 @@
         v((LON_BLOCKS, 128), F32),
         v((8, 128), F32),
         v((8, 128), F32),
-        v((512, 128), F32),
+        v((4, 8, 128), F32),
+        v((128, 128), F32),
         *[v((2 * KEEP, HALF), F32)] * 2,
         *[v((2 * KEEP * BETAS, CH), F32)] * 6,
         dma(6),

time: 120 us -> 114 us (0.950)
  Pallas kernels: 119 us -> 113 us
    pallas_call x1, Pallas kernels: 115 us -> 110 us  [body(): pl.pallas_call(functools.partial(kernel, fwd_scale, syn_scale), out_shape...]
where the time goes in v7:
time: 114 us
  Pallas kernels  113 us (99%)
    pallas_call x1, Pallas kernels, body(): pl.pallas_call(functools.partial(kernel, fwd_scale, syn_scale), out_shape...  110 us
    pallas_call x1, Pallas kernels, result_call(): pl.pallas_call(result_kernel, grid=(blocks,), out_shape=(jax.ShapeDtypeSt...  3.29 us

profile of v7, /device:TPU:0, one launch (start us, length us, event | category | flops | bytes accessed | tf_op | source)
XLA Modules:
  0.0 113.7 jit_solution(14039380638187926367)
XLA Ops:
  0.6 109.7 %layer_gradients.1 = (bf16[45,64,256]{2,1,0:T(8,128)(2,1)}, f32[32,2,16,256]{3,2,1,0:T(8,128)}) custom-call(bf16[45,64,256]{2,1,0:T(8,128)(2,1)} %bitcast.13, bf16[45,64,256]{2,1,0:T(8,128)(2,1)} %bitcast.11, bf16[32,2,16,256]{3,2,1,0:T(8,128)(2,1)} %refs_2_.1, bf16[256,1024]{1,0:T(8,128)(2,1)} %refs_3_.1, bf16[1024,256]{1,0:T(8,128)(2,1)} %refs_4_.1, ...), custom_call_target="tpu_custom_call" | custom-call | tf_op jit(solution)/shard_map/layer_gradients/pallas_call | solution.py:868
  110.4 3.3 %results.1 = (bf16[2880,256]{1,0:T(8,128)(2,1)}, f32[1024,256]{1,0:T(8,128)}) custom-call(bf16[2880,256]{1,0:T(8,128)(2,1)} %bitcast.12, bf16[2880,256]{1,0:T(8,128)(2,1)} %bitcast.14, f32[1024,256]{1,0:T(8,128)} %bitcast.15), custom_call_target="tpu_custom_call" | custom-call | tf_op jit(solution)/shard_map/results/pallas_call | solution.py:815

commit v8 on v7

--- a/solution.py
+++ b/solution.py
@@ -74,7 +74,7 @@
         dst_ref=dst,
         send_sem=sems[0],
         recv_sem=sems[1],
-        device_id=device_of(target),
+        device_id=target,
         device_id_type=MESH,
     )
     copy.start()
@@ -96,14 +96,42 @@
     return values[0] + (values[1] - values[0]) * core
 
 
-def piece_index(at, core, orders, depth=3):
-    return by_core(core, [index_of(at, order[:depth]) for order in orders])
+def once(at, key, work):
+    if key not in at["known"]:
+        at["known"][key] = work()
+    return at["known"][key]
+
+
+def place_on(at, axis, step):
+    return once(at, (axis, step), lambda: lax.rem(at[axis] + step, RING))
+
+
+def piece_index(at, orders, depth=3, own=True):
+    def work():
+        core = at["core"] if own else 1 - at["core"]
+        return by_core(core, [index_of(at, order[:depth]) for order in orders])
+
+    return once(at, (orders, depth, own), work)
+
+
+def piece_place(at, orders, depth, step, own=True):
+    def work():
+        core = at["core"] if own else 1 - at["core"]
+        return by_core(core, [place_on(at, order[depth], step) for order in orders])
+
+    return once(at, (orders, depth, step, own), work)
 
 
 def along(at, orders, depth, step):
-    moves = [moved(at, order[depth], step) for order in orders]
-    there = {name: by_core(at["core"], [move[name] for move in moves]) for name in "xyz"}
-    return {**there, "core": at["core"]}
+    def work():
+        devices = [device_of(moved(at, order[depth], step)) for order in orders]
+        return tuple(by_core(at["core"], pair) for pair in zip(*devices, strict=True))
+
+    return once(at, (orders, depth, step, "device"), work)
+
+
+def other_core(at):
+    return once(at, "other", lambda: device_of(moved(at, "core", 1)))
 
 
 def wait_bytes(ref, sem):
@@ -121,11 +149,11 @@
 def gather(at, pieces, full, sems):
     sent, recv, far_recv, core_recv = sems
     core = at["core"]
-    sibling = moved(at, "core", 1)
+    sibling = other_core(at)
 
     def slab(i, step, first, count):
         size, orders = pieces[i]
-        place = lax.rem(piece_index(at, core, orders, 1) + step, RING)
+        place = piece_place(at, orders, 0, step)
         start = core * (64 * size) + place * (16 * size) + first * (8 * size)
         return full[i].at[rows(start, count * (8 * size))]
 
@@ -138,7 +166,7 @@
             if phase:
                 wait_bytes(full[i].at[0 : 3 * size], recv.at[i, 0])
             block = size * RING**phase
-            index = piece_index(at, core, orders, 3 - phase)
+            index = piece_index(at, orders, 3 - phase)
             here = full[i].at[rows(core * (64 * size) + index * block, block)]
             for step in STEPS:
                 give(i, here, recv.at[i, phase], along(at, orders, 2 - phase, step))
@@ -196,15 +224,15 @@
     sent, core_recv, recv = scratch[:3]
     bufs = [scratch[3 + 8 * i : 11 + 8 * i] for i in range(3)]
     core = at["core"]
-    sibling = moved(at, "core", 1)
-
-    def slab(i, owner, step):
+    sibling = other_core(at)
+
+    def slab(i, own, step):
         size, orders = pieces[i]
-        return lax.rem(piece_index(at, owner, orders, 1) + step, RING) * (16 * size)
+        return piece_place(at, orders, 0, step, own) * (16 * size)
 
     for s, step in enumerate((2, 1, 3, 0)):
         for i, (size, orders) in enumerate(pieces):
-            start = slab(i, 1 - core, step)
+            start = slab(i, False, step)
             send(
                 parts[i].at[rows((1 - core) * (64 * size) + start, 16 * size)],
                 bufs[i][0].at[rows(start, 16 * size)],
@@ -215,14 +243,14 @@
 
     def give(i, step, first, kind, dst, target):
         size, _ = pieces[i]
-        here = rows(slab(i, core, step) + first * (8 * size), 8 * size)
+        here = rows(slab(i, True, step) + first * (8 * size), 8 * size)
         send(bufs[i][1].at[here], dst, (sent.at[i], recv.at[i, kind]), target)
 
     for s, step in enumerate((2, 1, 3, 0)):
         for i, (size, orders) in enumerate(pieces):
             sib, total, onward, landed = bufs[i][:4]
             right, left = along(at, orders, 0, 1), along(at, orders, 0, 3)
-            start = slab(i, core, step)
+            start = slab(i, True, step)
             here = rows(start, 16 * size)
             wait_bytes(sib.at[here], core_recv.at[i, s])
             mine = parts[i][rows(core * (64 * size) + start, 16 * size), :]
@@ -240,7 +268,7 @@
         _, total, onward, landed = bufs[i][:4]
         wait_bytes(onward, recv.at[i, 0])
         for way, (step, first) in enumerate(((1, 0), (3, 1))):
-            here = rows(slab(i, core, step) + first * (8 * size), 8 * size)
+            here = rows(slab(i, True, step) + first * (8 * size), 8 * size)
             total[here, :] = total[here, :] + onward[way]
             dst = landed.at[way, first * (8 * size) : (first + 1) * (8 * size)]
             give(i, step, first, 1, dst, along(at, orders, 0, step))
@@ -251,7 +279,7 @@
             mine, landed = ((1, 3), (4, 5), (6, 7))[phase]
             mine, landed = bufs[i][mine], bufs[i][landed]
             block = size * RING ** (2 - phase)
-            place = by_core(core, [at[order[phase]] for order in orders])
+            place = piece_place(at, orders, phase, 0)
             total = mine[rows(place * block, block), :].astype(F32)
             wait_bytes(landed, recv.at[i, phase + 1])
             for s in range(landed.shape[0]):
@@ -263,10 +291,9 @@
             after, there = bufs[i][4 + 2 * phase], bufs[i][5 + 2 * phase]
             after[...] = total.astype(BF16)
             small = block // RING
-            place = by_core(core, [at[order[phase + 1]] for order in orders])
             for s, step in enumerate(STEPS):
                 send(
-                    after.at[rows(lax.rem(place + step, RING) * small, small)],
+                    after.at[rows(piece_place(at, orders, phase + 1, step) * small, small)],
                     there.at[s],
                     (sent.at[i], recv.at[i, phase + 2]),
                     along(at, orders, phase + 1, step),
@@ -278,7 +305,7 @@
 def put_own(at, pieces, modes, full):
     first = 0
     for i, (size, orders) in enumerate(pieces):
-        here = rows((at["core"] * 64 + piece_index(at, at["core"], orders)) * size, size)
+        here = rows((at["core"] * 64 + piece_index(at, orders)) * size, size)
         full[i][here, :] = modes[first : first + size]
         first += size
 
@@ -296,7 +323,7 @@
 
 def gather_slots(at, own, other, line, full, sems):
     sems, past = sems
-    copy = send(own, other, (sems.at[0], sems.at[1]), moved(at, "core", 1))
+    copy = send(own, other, (sems.at[0], sems.at[1]), other_core(at))
     for step in STEPS:
         pl.semaphore_signal(
             past, inc=1, device_id=device_of(moved(at, "y", step)), device_id_type=MESH
@@ -306,7 +333,7 @@
     both_cores = own[...] + other[...]
     line[3] = both_cores
     for s, step in enumerate(STEPS):
-        send(line.at[3], line.at[s], (sems.at[2], sems.at[3]), moved(at, "x", step))
+        send(line.at[3], line.at[s], (sems.at[2], sems.at[3]), device_of(moved(at, "x", step)))
     yield
     wait_bytes(line.at[0:3], sems.at[3])
     pl.semaphore_wait(past, len(STEPS))
@@ -315,7 +342,12 @@
     for step in STEPS:
         ways += [(step, 0), (0, step)]
     for dy, dz in ways:
-        send(mine, mine, (sems.at[4], sems.at[5]), moved(moved(at, "y", dy), "z", dz))
+        send(
+            mine,
+            mine,
+            (sems.at[4], sems.at[5]),
+            device_of(moved(moved(at, "y", dy), "z", dz)),
+        )
     yield
     wait_bytes(full.at[0:120], sems.at[5])
     yield
@@ -439,7 +471,7 @@
                 store_modes(b, part, here, HALVES[h], parts[h])
         return carry
 
-    lax.fori_loop(0, LON_BLOCKS, one, 0, unroll=U_BLK)
+    lax.fori_loop(0, LON_BLOCKS, one, 0, unroll=U_HALF_BLK)
 
 
 def build_analysis(slots, table, out, low, high):
@@ -632,7 +664,7 @@
     scatter = [take(27), take(27)]
     analysis, synthesis = tables.at[0:8192], tables.at[8192:16384]
 
-    at = own_place()
+    at = {**own_place(), "known": {}}
     lat, lon = lax.axis_index("lat"), lax.axis_index("lon")
     greeted = greet(at)
     loads = []
@@ -730,8 +762,9 @@
             copy.wait()
         widen_weight(weight, weights)
 
-    work = [[prepare]]
-    for count in (3, 2, 2, 1, 2, 1, 2):
+    tasks.insert(0, prepare)
+    work = [[]]
+    for count in (3, 3, 2, 1, 2, 1, 2):
         work.append(tasks[:count])
         del tasks[:count]
     drive(*[exchange(h, fwd_scale, False, syn_scale) for h in range(2)], work)

time: 114 us -> 113 us (level)
    pallas_call x1, Pallas kernels: 110 us -> 109 us  [body(): pl.pallas_call(functools.partial(kernel, fwd_scale, syn_scale), out_shape...]
where the time goes in v8:
time: 113 us; the launch traced here: 112 us
  Pallas kernels  112 us (99%)
    pallas_call x1, Pallas kernels, body(): pl.pallas_call(functools.partial(kernel, fwd_scale, syn_scale), out_shape...  109 us
    pallas_call x1, Pallas kernels, result_call(): pl.pallas_call(result_kernel, grid=(blocks,), out_shape=(jax.ShapeDtypeSt...  3.29 us

profile of v8, /device:TPU:0, one launch (start us, length us, event | category | flops | bytes accessed | tf_op | source)
XLA Modules:
  0.0 112.5 jit_solution(6713009564257149245)
XLA Ops:
  0.6 108.6 %layer_gradients.1 = (bf16[45,64,256]{2,1,0:T(8,128)(2,1)}, f32[32,2,16,256]{3,2,1,0:T(8,128)}) custom-call(bf16[45,64,256]{2,1,0:T(8,128)(2,1)} %bitcast.13, bf16[45,64,256]{2,1,0:T(8,128)(2,1)} %bitcast.11, bf16[32,2,16,256]{3,2,1,0:T(8,128)(2,1)} %refs_2_.1, bf16[256,1024]{1,0:T(8,128)(2,1)} %refs_3_.1, bf16[1024,256]{1,0:T(8,128)(2,1)} %refs_4_.1, ...), custom_call_target="tpu_custom_call" | custom-call | tf_op jit(solution)/shard_map/layer_gradients/pallas_call | solution.py:901
  109.2 3.3 %results.1 = (bf16[2880,256]{1,0:T(8,128)(2,1)}, f32[1024,256]{1,0:T(8,128)}) custom-call(bf16[2880,256]{1,0:T(8,128)(2,1)} %bitcast.12, bf16[2880,256]{1,0:T(8,128)(2,1)} %bitcast.14, f32[1024,256]{1,0:T(8,128)} %bitcast.15), custom_call_target="tpu_custom_call" | custom-call | tf_op jit(solution)/shard_map/results/pallas_call | solution.py:848

commit v9 on v8

--- a/solution.py
+++ b/solution.py
@@ -29,7 +29,7 @@
 F32, BF16 = jnp.float32, jnp.bfloat16
 VMEM = pl.BlockSpec(memory_space=pltpu.VMEM)
 LIMIT = 60 << 20
-U_FILL, U_ROW, U_BLK, U_BUILD, GROUP, CHUNK = 5, 16, 8, 4, 9, 256
+U_FILL, U_ROW, U_BLK, U_BUILD, GROUP, CHUNK = 15, 16, 8, 8, 9, 256
 U_HALF_ROW, U_HALF_BLK = 64, 32
 
 
@@ -567,7 +567,7 @@
                 ]
         return carry
 
-    lax.fori_loop(low, high, one, 0)
+    lax.fori_loop(low, high, one, 0, unroll=high - low)
 
 
 BETAS = HALF // BS

time: 113 us -> 111 us (0.982)
  Pallas kernels: 112 us -> 110 us
    pallas_call x1, Pallas kernels: 109 us -> 107 us  [body(): pl.pallas_call(functools.partial(kernel, fwd_scale, syn_scale), out_shape...]
where the time goes in v9:
time: 111 us
  Pallas kernels  110 us (99%)
    pallas_call x1, Pallas kernels, body(): pl.pallas_call(functools.partial(kernel, fwd_scale, syn_scale), out_shape...  107 us
    pallas_call x1, Pallas kernels, result_call(): pl.pallas_call(result_kernel, grid=(blocks,), out_shape=(jax.ShapeDtypeSt...  3.29 us

profile of v9, /device:TPU:0, one launch (start us, length us, event | category | flops | bytes accessed | tf_op | source)
XLA Modules:
  0.0 111.1 jit_solution(5276134083512889924)
XLA Ops:
  0.6 107.2 %layer_gradients.1 = (bf16[45,64,256]{2,1,0:T(8,128)(2,1)}, f32[32,2,16,256]{3,2,1,0:T(8,128)}) custom-call(bf16[45,64,256]{2,1,0:T(8,128)(2,1)} %bitcast.13, bf16[45,64,256]{2,1,0:T(8,128)(2,1)} %bitcast.11, bf16[32,2,16,256]{3,2,1,0:T(8,128)(2,1)} %refs_2_.1, bf16[256,1024]{1,0:T(8,128)(2,1)} %refs_3_.1, bf16[1024,256]{1,0:T(8,128)(2,1)} %refs_4_.1, ...), custom_call_target="tpu_custom_call" | custom-call | tf_op jit(solution)/shard_map/layer_gradients/pallas_call | solution.py:901
  107.8 3.3 %results.1 = (bf16[2880,256]{1,0:T(8,128)(2,1)}, f32[1024,256]{1,0:T(8,128)}) custom-call(bf16[2880,256]{1,0:T(8,128)(2,1)} %bitcast.12, bf16[2880,256]{1,0:T(8,128)(2,1)} %bitcast.14, f32[1024,256]{1,0:T(8,128)} %bitcast.15), custom_call_target="tpu_custom_call" | custom-call | tf_op jit(solution)/shard_map/results/pallas_call | solution.py:848
